TPU v7x, 32 devices: a whole 2x2x4 slice. The times are simulated.
32 devices in a mesh: dp: 8 (over z, x), mp: 4 (over y, core).
Axes of the slice: x: 2, y: 2, z: 4, core: 2. Of those that a mesh axis runs over, the one named last changes fastest.
Arguments:
- block_input: bfloat16 [8, 8192, 512], P('dp', 'mp'), may hold values from -6 to 6
- routes: int32 [8, 8192, 2], P('dp', 'mp'), may hold values from 0 to 7, all different within a row; in each aligned block of 2048 rows (0 to 2047, 2048 to 4095, ..., all dimensions but the last counted through in order) at most 1024 rows name the same one
- lengths: int32 [8], P('dp'), may hold values from 6145 to 8192, as said below
- first_gain: float32 [512], replicated, may hold values from 0.25 to 1.75
- first_bias: float32 [512], replicated, may hold values from -1.5 to 1.5
- router_weight: bfloat16 [512, 8], replicated, may hold values from -0.1875 to 0.1875
- shared_proj: bfloat16 [512, 128], replicated, may hold values from -0.25 to 0.25
- query_weight: bfloat16 [64, 4096], P('mp', 'dp'), may hold values from -0.25 to 0.25
- output_weight: bfloat16 [64, 4096], P('mp', 'dp'), may hold values from -40 to 40
- second_gain: float32 [512], replicated, may hold values from 0.25 to 1.75
- second_bias: float32 [512], replicated, may hold values from -1.5 to 1.5
- expand_weight: bfloat16 [512, 2048], P(None, 'mp'), may hold values from -0.25 to 0.25
- expand_bias: bfloat16 [2048], P('mp'), may hold values from -1.5 to 1.5
- reduce_weight: bfloat16 [2048, 512], P('mp'), may hold values from -0.125 to 0.125
- reduce_bias: bfloat16 [512], replicated, may hold values from -1.5 to 1.5
- upstream_grad: bfloat16 [8, 8192, 512], P('dp', 'mp'), may hold values from -6 to 6
Outputs:
- block_output: bfloat16 [8, 8192, 512], P('dp', 'mp')
- input_grad: float32 [8, 8192, 512], P('dp', 'mp')
- first_gain_grad: float32 [512], P('mp')
- first_bias_grad: float32 [512], P('mp')
- router_grad: float32 [512, 8], P('mp')
- shared_grad: float32 [512, 128], P('mp')
- query_weight_grad: float32 [64, 4096], P('mp', 'dp')
- output_weight_grad: float32 [64, 4096], P('mp', 'dp')
- second_gain_grad: float32 [512], P('mp')
- second_bias_grad: float32 [512], P('mp')
- expand_weight_grad: float32 [512, 2048], P(None, 'mp')
- expand_bias_grad: float32 [2048], P('mp')
- reduce_weight_grad: float32 [2048, 512], P('mp')
- reduce_bias_grad: float32 [512], P('mp')
Inputs may be any that keep to these rules, and one draw needn't show every extreme that they name: `routes`: the two experts of a position differ. In each aligned block of 2048 positions of a sequence, no expert is named by more than 1024 positions, a bound that some block reaches. `lengths`: one sequence has length 8192 and another 3 * 2048 + 1.
All inputs are finite; a program needn't handle non-finite values.
Results may differ from a plain program's by a relative error of at most 0.013.
Values may be sent and summed in bfloat16 or wider, within the bound.
No kernel may reach another device: no remote copies, remote signals or barrier semaphores. Data moves between devices by JAX's collectives and lax.ppermute only.
A program may use at most 256 MiB of HBM per device.

v0:
```python
import functools

import jax
import jax.numpy as jnp
from jax import lax
from jax.experimental import pallas as pl
from jax.experimental.pallas import tpu as pltpu
from jax.sharding import PartitionSpec as P

F32 = jnp.float32
BF = jnp.bfloat16
EPS = 1e-05
LOG2E = 1.4426950408889634
LN2 = 0.6931471805599453
MASKED = -1e30
GELU_A = 0.7978845608028654
GELU_B = 0.044715
SAFE = 60.0
LANES = 128


def nn(a, b):
    return lax.dot_general(a, b, (((1,), (0,)), ((), ())), preferred_element_type=F32)


def nt(a, b):
    return lax.dot_general(a, b, (((1,), (1,)), ((), ())), preferred_element_type=F32)


def tn(a, b):
    return lax.dot_general(a, b, (((0,), (0,)), ((), ())), preferred_element_type=F32)


def norm_parts(values):
    centred = values - jnp.mean(values, axis=-1, keepdims=True)
    inverse = lax.rsqrt(jnp.mean(centred * centred, axis=-1, keepdims=True) + EPS)
    return centred * inverse, inverse


def norm_back(grad, normal, inverse, gain):
    scaled = grad * gain
    return inverse * (
        scaled
        - jnp.mean(scaled, axis=-1, keepdims=True)
        - normal * jnp.mean(scaled * normal, axis=-1, keepdims=True)
    )


def three(value):
    high = value.astype(BF).astype(F32)
    rest = value - high
    middle = rest.astype(BF).astype(F32)
    return high, middle, rest - middle


def extra_rows(value, last):
    row = lax.broadcasted_iota(jnp.int32, (16, value.shape[1]), 0)
    high, middle, low = three(value)
    out = jnp.where(row == 0, -high, 0.0)
    out = jnp.where(row == 1, -middle, out)
    out = jnp.where(row == 2, -low, out)
    return jnp.where(row == 3, last, out)


def spread(first, second, route0, route1, experts):
    zero = jnp.zeros_like(first)
    return jnp.concatenate(
        [
            jnp.where(route0 == e, first, jnp.where(route1 == e, second, zero))
            for e in range(experts)
        ],
        axis=0,
    )


def picked(table, route, experts):
    head = table.shape[0] // experts
    out = jnp.zeros((head, table.shape[1]), F32)
    for e in range(experts):
        out = jnp.where(route == e, table[e * head : (e + 1) * head, :], out)
    return out


def key_rows(pair, live, head):
    lane = lax.broadcasted_iota(jnp.int32, pair.shape, 1)
    row = lax.broadcasted_iota(jnp.int32, pair.shape, 0)
    ones = jnp.where(lane < head + 3, 1.0, 0.0)
    mask = jnp.where(row < live, 0.0, MASKED)
    out = jnp.where(lane == head + 3, mask, ones)
    return jnp.where(lane < head, pair.astype(F32), out).astype(BF)


def first_kernel(x, gain, bias, router, proj, routes, normed, pairs, gates):
    experts = router.shape[0] // 2
    normal, _ = norm_parts(x[...].astype(F32))
    out = (normal * gain[...] + bias[...]).astype(BF)
    normed[...] = out
    pairs[...] = nn(out, proj[...]).astype(BF)
    logits = nt(router[...], out)
    route = routes[...]
    chosen = []
    for s in range(2):
        one = jnp.zeros((1, logits.shape[1]), F32)
        for e in range(experts):
            one = jnp.where(route[s : s + 1, :] == e, logits[e : e + 1, :], one)
        chosen.append(one)
    top = jnp.maximum(chosen[0], chosen[1])
    up0, up1 = jnp.exp(chosen[0] - top), jnp.exp(chosen[1] - top)
    inverse = 1.0 / (up0 + up1)
    gates[0:1, :] = up0 * inverse
    gates[1:2, :] = up1 * inverse


def assembled(table, shares, where, experts, start):
    head = table.shape[0] // experts
    share = head // 4
    for o, part in enumerate(shares):
        for e in range(experts):
            at = pl.multiple_of(e * head + where[o] * share, share)
            here = slice(start + e * share, start + (e + 1) * share)
            table[pl.ds(at, share), :] = part[here, :]


def query_kernel(where, normed, t0, t1, t2, t3, routes, queries, q_rows, table, *, experts, scale):
    @pl.when(pl.program_id(0) == 0)
    def _():
        assembled(table, (t0, t1, t2, t3), where, experts, 0)

    every = nt(table[...], normed[...]) * scale
    for s in range(2):
        one = picked(every, routes[s : s + 1, :], experts)
        queries[s] = one.astype(BF)
        q_rows[s] = jnp.concatenate([one, jnp.zeros_like(one)], axis=0).T.astype(BF)


def attend_kernel(live, q, p0, p1, p2, p3, out, kept, keys, values, limit, top, *, head, span):
    part = p0.shape[0]

    @pl.when((pl.program_id(0) == 0) & (pl.program_id(1) == 0))
    def _():
        row = lax.broadcasted_iota(jnp.int32, (LANES, LANES), 0)
        col = lax.broadcasted_iota(jnp.int32, (LANES, LANES), 1)
        move = jnp.where((col == row + head) & (row < head), 1.0, 0.0).astype(BF)
        count = jnp.where(row < head, 1.0, 0.0).astype(BF)
        longest = jnp.zeros((1, LANES), F32)
        for o, p in enumerate((p0, p1, p2, p3)):
            pair = p[...]
            keys[o * part : (o + 1) * part, :] = key_rows(pair, live[o], head)
            turned = nt(move, pair)
            line = lax.broadcasted_iota(jnp.int32, turned.shape, 0)
            values[:, o * part : (o + 1) * part] = jnp.where(line == head, 1.0, turned).astype(BF)
            wide = pair.astype(F32)
            squares = nn((wide * wide).astype(BF), count)
            longest = jnp.maximum(longest, jnp.max(squares, axis=0, keepdims=True))
        limit[...] = jnp.broadcast_to(1.02 * jnp.sqrt(longest), limit.shape)

    query = q[0]
    wide = query.astype(F32)
    length = jnp.sqrt(jnp.sum(wide * wide, axis=0, keepdims=True))
    bound = length * limit[0:1, 0:1]
    top[...] = jnp.zeros_like(top)
    n = query.shape[1]
    rest = jnp.zeros((LANES - head - 16, n), BF)

    @pl.when(jnp.max(bound) > SAFE)
    def _():
        plain = jnp.concatenate(
            [query, extra_rows(jnp.zeros((1, n), F32), 1.0).astype(BF), rest], axis=0
        )

        def peak(j, now):
            at = pl.multiple_of(j * 512, 512)
            scores = nn(keys[pl.ds(at, 512), :], plain)
            return jnp.maximum(now, jnp.max(scores, axis=0, keepdims=True))

        best = lax.fori_loop(0, 4 * part // 512, peak, jnp.full((1, n), -3e38, F32))
        top[...] = jnp.broadcast_to(best, top.shape)

    extended = jnp.concatenate([query, extra_rows(top[0:1, :], 1.0).astype(BF), rest], axis=0)
    total = jnp.zeros((LANES, n), F32)
    for j in range(4 * part // span):
        here = slice(j * span, (j + 1) * span)
        weights = jnp.exp2(nn(keys[here, :], extended)).astype(BF)
        kept[here, :] = weights
        total = total + nn(values[:, here], weights)
    inverse = 1.0 / total[head : head + 1, :]
    out[0, 0:head, :] = total[0:head, :] * inverse
    out[0, head : head + 8, :] = jnp.broadcast_to(inverse, (8, n))


def attend_back_kernel(dot, do, q, *rest, head, places, first):
    if not first:
        before, *rest = rest
    pieces = len(places)
    weights, pairs, after = rest[:pieces], rest[pieces : 2 * pieces], rest[2 * pieces]
    grads = rest[2 * pieces + 1 : 3 * pieces + 1]
    values, turned, both = rest[3 * pieces + 1 :]
    step = pl.program_id(0)
    sizes = [pair.shape[0] for pair in pairs]
    spans = [slice(sum(sizes[:n]), sum(sizes[: n + 1])) for n in range(pieces)]

    @pl.when(step == 0)
    def _():
        row = lax.broadcasted_iota(jnp.int32, (head, LANES), 0)
        col = lax.broadcasted_iota(jnp.int32, (head, LANES), 1)
        same = jnp.where(row == col, 1.0, 0.0).astype(BF)
        for pair, here in zip(pairs, spans):
            rows = pair[...]
            turned[:, here] = nt(same, rows).astype(BF)
            lane = lax.broadcasted_iota(jnp.int32, rows.shape, 1)
            fixed = jnp.where(lane < 3, 1.0, 0.0)
            values[here, :] = jnp.where(lane < head, fixed, rows.astype(F32)).astype(BF)
        both[...] = jnp.zeros_like(both)

    right = jnp.concatenate([q[0], do[0]], axis=0)
    grown = jnp.zeros((head, q.shape[1]), F32)
    for weight, here in zip(weights, spans):
        attention = weight[...]
        scores = (attention.astype(F32) * nn(values[here, :], dot[0])).astype(BF)
        both[here, :] += nn(jnp.concatenate([scores, attention], axis=1), right)
        grown = grown + nn(turned[:, here], scores)
    after[0] = grown if first else before[0] + grown

    @pl.when(step == pl.num_programs(0) - 1)
    def _():
        for grad, here in zip(grads, spans):
            lane = lax.broadcasted_iota(jnp.int32, grad.shape, 1)
            grad[...] = (both[here, :] * jnp.where(lane < head, LN2, 1.0)).astype(BF)


def middle_kernel(
    where, att, routes, gates, x, up, normed,
    f0, f1, f2, f3, rb, gain, bias,
    out, mid_grad, do_rows, do_t, logit, g0, g1, g2, g3,
    we_sum, wr_sum, wo_sum, eb_sum, small, rt_sum, wo,
    *, head, experts,
):
    step = pl.program_id(0)

    @pl.when(step == 0)
    def _():
        for r in (we_sum, wr_sum, wo_sum, eb_sum, small, rt_sum):
            r[...] = jnp.zeros_like(r)
        assembled(wo, (f0, f1, f2, f3), where, experts, f0.shape[0] - experts * (head // 4))

    route0, route1 = routes[0:1, :], routes[1:2, :]
    gate0, gate1 = gates[0:1, :], gates[1:2, :]
    mix0, mix1 = att[0, 0:head, :], att[1, 0:head, :]
    low0, low1 = mix0.astype(BF).astype(F32), mix1.astype(BF).astype(F32)
    mixed = spread(gate0 * low0, gate1 * low1, route0, route1, experts).astype(BF)
    middle = x[...].astype(F32) + tn(mixed, wo[...])
    normal, inverse = norm_parts(middle)
    normed_two = (normal * gain[...] + bias[...]).astype(BF)
    upstream = up[...]
    n2t = normed_two.T
    upt = upstream.T
    ff = f0.shape[1]
    width = middle.shape[1]
    reduced = jnp.zeros(middle.shape, F32)
    two_grad = jnp.zeros(middle.shape, F32)
    for o, f in enumerate((f0, f1, f2, f3)):
        here = slice(o * ff, (o + 1) * ff)
        we, wr = f[0:width, :], f[width : width + ff, :]
        v = nn(normed_two, we) + f[width + ff : width + ff + 16, :].astype(F32)[0:1, :]
        square = v * v
        inner = v * (GELU_A + (GELU_A * GELU_B) * square)
        half = 0.5 + 0.5 * jnp.tanh(inner)
        act = v * half
        slope = half + 2.0 * act * (1.0 - half) * (GELU_A + (3.0 * GELU_A * GELU_B) * square)
        low = act.astype(BF)
        reduced = reduced + nn(low, wr)
        back = nt(upstream, wr) * slope
        back_low = back.astype(BF)
        two_grad = two_grad + nt(back_low, we)
        we_sum[:, here] += nn(n2t, back_low)
        wr_sum[:, here] += nn(upt, low)
        eb_sum[0:1, here] += jnp.sum(back_low.astype(F32), axis=0, keepdims=True)
    out[...] = (middle + reduced + rb[...]).astype(BF)
    wide_up = upstream.astype(F32)
    mid = wide_up + norm_back(two_grad, normal, inverse, gain[...])
    mid_grad[...] = mid
    small[0:1, :] += jnp.sum(wide_up, axis=0, keepdims=True)
    small[1:2, :] += jnp.sum(two_grad * normal, axis=0, keepdims=True)
    small[2:3, :] += jnp.sum(two_grad, axis=0, keepdims=True)
    mid_low = mid.astype(BF)
    wo_sum[...] += nn(mixed, mid_low)
    every = nt(wo[...], mid_low)
    pull0, pull1 = picked(every, route0, experts), picked(every, route1, experts)
    gate_grad0 = jnp.sum(low0 * pull0, axis=0, keepdims=True)
    gate_grad1 = jnp.sum(low1 * pull1, axis=0, keepdims=True)
    both = gate0 * gate_grad0 + gate1 * gate_grad1
    chosen0, chosen1 = gate0 * (gate_grad0 - both), gate1 * (gate_grad1 - both)
    row = lax.broadcasted_iota(jnp.int32, (16, chosen0.shape[1]), 0)
    logit_rows = jnp.where(row == route0, chosen0, jnp.where(row == route1, chosen1, 0.0))
    logit_high = logit_rows.astype(BF)
    logit_low = (logit_rows - logit_high.astype(F32)).astype(BF)
    logit[...] = logit_high
    here_normed = normed[...]
    rt_sum[...] += nn(logit_high, here_normed) + nn(logit_low, here_normed)
    rest = jnp.zeros((LANES - head - 16, row.shape[1]), F32)
    for s, (gate, pull, mix) in enumerate(((gate0, pull0, mix0), (gate1, pull1, mix1))):
        low = (gate * pull * att[s, head : head + 1, :]).astype(BF)
        grad = low.astype(F32)
        delta = jnp.sum(grad * mix, axis=0, keepdims=True)
        do_t[s] = jnp.concatenate([extra_rows(delta, 0.0), rest, grad], axis=0).astype(BF)
        do_rows[s] = jnp.concatenate([jnp.zeros_like(grad), grad], axis=0).T.astype(BF)

    @pl.when(step == pl.num_programs(0) - 1)
    def _():
        share = head // 4
        table = g0.shape[0] - experts * share
        for o, g in enumerate((g0, g1, g2, g3)):
            here = slice(o * ff, (o + 1) * ff)
            g[0:width, :] = we_sum[:, here].astype(BF)
            g[width : 2 * width, :] = wr_sum[:, here].astype(BF)
            line = lax.broadcasted_iota(jnp.int32, (8, ff), 0)
            head_rows = jnp.where(line == 3, eb_sum[0:1, here], small[...])
            g[2 * width : 2 * width + 16, :] = jnp.concatenate(
                [head_rows, rt_sum[0:8, :]], axis=0
            ).astype(BF)
            g[2 * width + 16 : table, :] = jnp.zeros((table - 2 * width - 16, ff), BF)
            for e in range(experts):
                at = pl.multiple_of(e * head + where[o] * share, share)
                g[table + e * share : table + (e + 1) * share, :] = wo_sum[
                    pl.ds(at, share), :
                ].astype(BF)


def last_kernel(
    where, dq, pa, pd, p1, p2, p3, logit, routes, normed, x, mid_grad, gain, wq, proj, router,
    out, s0, s1, s2, s3, wq_sum, sp_sum, small, *, head, experts, scale,
):
    step = pl.program_id(0)

    @pl.when(step == 0)
    def _():
        for r in (wq_sum, sp_sum, small):
            r[...] = jnp.zeros_like(r)

    route0, route1 = routes[0:1, :], routes[1:2, :]
    grad0, grad1 = dq[0] * scale, dq[1] * scale
    placed = spread(grad0, grad1, route0, route1, experts).astype(BF)
    own = jnp.where(step < pl.num_programs(0) // 2, pa[...].astype(F32), pd[...].astype(F32))
    for p in (p1, p2, p3):
        own = own + p[...].astype(F32)
    pair = own.astype(BF)
    normed_grad = tn(placed, wq[...]) + nt(pair, proj[...]) + tn(logit[...], router[...])
    here_normed = normed[...]
    wq_sum[...] += nn(placed, here_normed)
    sp_sum[...] += tn(pair, here_normed)
    normal, inverse = norm_parts(x[...].astype(F32))
    out[...] = mid_grad[...] + norm_back(normed_grad, normal, inverse, gain[...])
    small[0:1, :] += jnp.sum(normed_grad * normal, axis=0, keepdims=True)
    small[1:2, :] += jnp.sum(normed_grad, axis=0, keepdims=True)

    @pl.when(step == pl.num_programs(0) - 1)
    def _():
        share = head // 4
        block = sp_sum.shape[1] // 4
        each = sp_sum.shape[0] // 4
        table = experts * share
        for o, s in enumerate((s0, s1, s2, s3)):
            owner = where[o]
            for e in range(experts):
                at = pl.multiple_of(e * head + owner * share, share)
                s[e * share : (e + 1) * share, :] = wq_sum[pl.ds(at, share), :].astype(BF)
            lanes = pl.ds(pl.multiple_of(owner * block, block), block)
            s[table + each : table + each + 16, :] = jnp.zeros((16, 4 * block), BF)
            ends = jnp.concatenate([small[:, lanes], jnp.zeros((8, block), F32)], axis=0)
            s[table + each : table + each + 16, 0:block] = ends.astype(BF)
            for g in range(4):
                piece = sp_sum[g * each : (g + 1) * each, lanes]
                s[table : table + each, g * block : (g + 1) * block] = piece.astype(BF)


def swapped(value, bit):
    return lax.ppermute(value, "mp", [(i, i ^ bit) for i in range(4)])


def four(value):
    across = swapped(value, 2)
    return value, swapped(value, 1), across, swapped(across, 1)


def summed(a, b):
    return (a.astype(F32) + b.astype(F32)).astype(BF)


def group_sum(parts):
    far = summed(parts[2], swapped(parts[3], 1))
    near = summed(parts[0], swapped(parts[1], 1))
    return near, swapped(far, 2)


def sent_to_all(value, axes):
    n = lax.axis_size(axes)
    wide = jnp.broadcast_to(value[None], (n,) + value.shape)
    return lax.all_to_all(wide, axes, split_axis=0, concat_axis=0, tiled=True)


def spec(shape, index):
    return pl.BlockSpec(shape, index)


def fixed(shape):
    return pl.BlockSpec(shape, lambda *_: (0,) * len(shape))


def shape(dims, kind):
    return jax.ShapeDtypeStruct(dims, kind)


SMEM = pl.BlockSpec(memory_space=pltpu.SMEM)
PARAMS = pltpu.CompilerParams(vmem_limit_bytes=58 * 2**20)


def cost(us):
    return pl.CostEstimate(flops=int(us * 1.1e9), bytes_accessed=1024, transcendentals=0)


def tied(value, *others):
    return lax.optimization_barrier((value, *others))[0]


def on_device(
    block_input, routes, lengths, first_gain, first_bias, router_weight, shared_proj,
    query_weight, output_weight, second_gain, second_bias, expand_weight, expand_bias,
    reduce_weight, reduce_bias, upstream_grad,
):
    tokens, width = block_input.shape[1], block_input.shape[2]
    experts = router_weight.shape[1]
    head = query_weight.shape[0] * lax.axis_size("mp")
    dp = lax.axis_size("dp")
    units = expand_weight.shape[1]
    me = lax.axis_index("mp")
    owners = me ^ jnp.arange(4, dtype=jnp.int32)
    live = jnp.clip(lengths[0] - owners * tokens, 0, tokens)
    x = block_input.reshape(tokens, width)
    up = upstream_grad.reshape(tokens, width)
    routes_t = routes.reshape(tokens, 2).T
    router_t = jnp.concatenate([router_weight.T, jnp.zeros((experts, width), BF)], axis=0)
    gain1, bias1 = first_gain[None], first_bias[None]
    gain2, bias2 = second_gain[None], second_bias[None]

    tb = 512
    rows = spec((tb, width), lambda i: (i, 0))
    cols2 = spec((2, tb), lambda i: (0, i))
    normed, pairs, gates = pl.pallas_call(
        first_kernel,
        grid=(tokens // tb,),
        in_specs=[rows, fixed((1, width)), fixed((1, width)), fixed((2 * experts, width)),
                  fixed((width, 2 * head)), cols2],
        out_specs=[rows, spec((tb, 2 * head), lambda i: (i, 0)), cols2],
        out_shape=[shape((tokens, width), BF), shape((tokens, 2 * head), BF), shape((2, tokens), F32)],
        compiler_params=PARAMS,
        cost_estimate=cost(5),
    )(x, gain1, bias1, router_t, shared_proj, routes_t)

    pair_across = swapped(pairs, 2)
    pair_beside = swapped(pairs, 1)
    both = jnp.concatenate([query_weight, output_weight], axis=0)
    shares = sent_to_all(both, "dp")
    shares = shares.reshape(experts, dp // experts, 2, head // 4, -1).transpose(2, 0, 3, 1, 4)
    shares = shares.reshape(2, experts * head // 4, width)
    table = [shares[0]] + [swapped(shares[0], bit) for bit in (1, 2, 3)]
    feed = jnp.concatenate(
        [expand_weight, reduce_weight, jnp.broadcast_to(expand_bias[None], (16, units)), shares[1]],
        axis=0,
    )
    feed, pair_across = lax.optimization_barrier((feed, pair_across))
    pair = (pairs, pair_beside, pair_across, swapped(pair_across, 1))
    feed_across = swapped(feed, 2)
    queries, q_rows, wq = pl.pallas_call(
        functools.partial(query_kernel, experts=experts, scale=0.125 * LOG2E),
        grid=(tokens // tb,),
        in_specs=[SMEM, rows] + [fixed((experts * head // 4, width))] * 4 + [cols2],
        out_specs=[spec((2, head, tb), lambda i: (0, 0, i)), spec((2, tb, LANES), lambda i: (0, i, 0)),
                   fixed((experts * head, width))],
        out_shape=[shape((2, head, tokens), BF), shape((2, tokens, LANES), BF),
                   shape((experts * head, width), BF)],
        compiler_params=PARAMS,
        cost_estimate=cost(5),
    )(owners, normed, *table, routes_t)

    tq = 512
    att, kept = pl.pallas_call(
        functools.partial(attend_kernel, head=head, span=4 * tokens),
        grid=(2, tokens // tq),
        in_specs=[SMEM, spec((1, head, tq), lambda s, i: (s, 0, i))] + [fixed((tokens, 2 * head))] * 4,
        out_specs=[spec((1, head + 8, tq), lambda s, i: (s, 0, i)),
                   spec((4 * tokens, tq), lambda s, i: (0, s * (tokens // tq) + i))],
        out_shape=[shape((2, head + 8, tokens), F32), shape((4 * tokens, 2 * tokens), BF)],
        scratch_shapes=[
            pltpu.VMEM((4 * tokens, LANES), BF), pltpu.VMEM((LANES, 4 * tokens), BF),
            pltpu.VMEM((8, LANES), F32), pltpu.VMEM((8, tq), F32),
        ],
        compiler_params=PARAMS,
        cost_estimate=cost(33),
    )(live, queries, *pair)

    feed_across = tied(feed_across, att)
    feeds = (feed, swapped(feed, 1), feed_across, swapped(feed_across, 1))

    tm = 512
    rows = spec((tm, width), lambda i: (i, 0))
    cols2 = spec((2, tm), lambda i: (0, i))
    tail = 2 * width + 64
    share = experts * head // 4
    slot = tail + share
    both_rows = spec((2, tm, LANES), lambda i: (0, i, 0))
    both_cols = spec((2, LANES, tm), lambda i: (0, 0, i))
    att_cols = spec((2, head + 8, tm), lambda i: (0, 0, i))
    block_out, mid_grad, do_rows, do_t, logit, *ffn = pl.pallas_call(
        functools.partial(middle_kernel, head=head, experts=experts),
        grid=(tokens // tm,),
        in_specs=[SMEM, att_cols, cols2, cols2, rows, rows, rows]
        + [fixed(feed.shape)] * 4 + [fixed((1, width))] * 3,
        out_specs=[rows, rows, both_rows, both_cols, spec((16, tm), lambda i: (0, i))]
        + [fixed((slot, units))] * 4,
        out_shape=[shape((tokens, width), BF), shape((tokens, width), F32), shape((2, tokens, LANES), BF),
                   shape((2, LANES, tokens), BF), shape((16, tokens), BF)]
        + [shape((slot, units), BF)] * 4,
        scratch_shapes=[
            pltpu.VMEM((width, 4 * units), F32), pltpu.VMEM((width, 4 * units), F32),
            pltpu.VMEM((experts * head, width), F32), pltpu.VMEM((8, 4 * units), F32),
            pltpu.VMEM((8, width), F32), pltpu.VMEM((16, width), F32),
            pltpu.VMEM((experts * head, width), BF),
        ],
        compiler_params=PARAMS,
        cost_estimate=cost(50),
    )(owners, att, routes_t, gates, x, up, normed, *feeds, reduce_bias[None].astype(F32),
      gain2, bias2)

    def back_call(places, before, us):
        many = sum(size for _, _, size in places)
        first = before is None
        tq = 512
        per = tokens // tq
        row_block = spec((1, tq, LANES), lambda i: (i // per, i % per, 0))
        col_block = spec((1, LANES, tq), lambda i: (i // per, 0, i % per))
        grad_block = spec((1, head, tq), lambda i: (i // per, 0, i % per))
        return pl.pallas_call(
            functools.partial(attend_back_kernel, head=head, places=places, first=first),
            grid=(2 * per,),
            in_specs=[col_block, row_block, row_block] + [grad_block] * (not first)
            + [spec((size, tq), lambda i, at=o * tokens // size + at: (at, i)) for o, at, size in places]
            + [spec((size, 2 * head), lambda i, at=at: (at, 0)) for _, at, size in places],
            out_specs=[grad_block] + [fixed((size, 2 * head)) for _, _, size in places],
            out_shape=[shape((2, head, tokens), F32)]
            + [shape((size, 2 * head), BF) for _, _, size in places],
            input_output_aliases={} if first else {3: 0},
            scratch_shapes=[
                pltpu.VMEM((many, LANES), BF), pltpu.VMEM((head, many), BF),
                pltpu.VMEM((many, LANES), F32),
            ],
            compiler_params=PARAMS,
            cost_estimate=cost(us),
        )(do_t, do_rows, q_rows, *([] if first else [before]), *[kept] * len(places),
          *[pair[o] for o, _, _ in places])

    def by_holder(rows_of):
        each = rows_of.reshape(experts, head // 4, dp // experts, -1).transpose(0, 2, 1, 3)
        return each.reshape(dp, -1, width)

    half = tokens // 2
    arrived = [swapped(ffn[bit], bit) for bit in (3, 2, 1)]
    q_grad, key3, key2, key0a = back_call(
        [(3, 0, tokens), (2, 0, tokens), (0, 0, half)], None, 55
    )
    own = sum([a.astype(F32) for a in arrived], ffn[0].astype(F32)).astype(BF)
    own = jnp.concatenate([own[:tail].reshape(dp, -1, width), by_holder(own[tail:])], axis=1)
    q_grad, own, key3, key2 = lax.optimization_barrier((q_grad, own, key3, key2))
    key_from3, key_from2 = swapped(key3, 3), swapped(key2, 2)
    arrived = lax.all_to_all(own, "dp", split_axis=0, concat_axis=0, tiled=True)
    q_grad, key1, key0b = back_call([(1, 0, tokens), (0, 1, half)], q_grad, 35)
    piece = jnp.sum(arrived.astype(F32), axis=0)
    q_grad, piece, key1 = lax.optimization_barrier((q_grad, piece, key1))
    key_from1 = swapped(key1, 1)
    total = sent_to_all(piece[: tail // dp].astype(BF), "dp").reshape(tail, units)
    wo_total = piece[tail // dp :].reshape(head // 4, -1)

    tl = 512
    rows = spec((tl, width), lambda i: (i, 0))
    cols2 = spec((2, tl), lambda i: (0, i))
    pair_rows = spec((tl, 2 * head), lambda i: (i, 0))
    count = half // tl
    first_rows = spec((tl, 2 * head), lambda i: (jnp.minimum(i, count - 1), 0))
    second_rows = spec((tl, 2 * head), lambda i: (jnp.maximum(i - count, 0), 0))
    input_grad, *last = pl.pallas_call(
        functools.partial(last_kernel, head=head, experts=experts, scale=0.125),
        grid=(tokens // tl,),
        in_specs=[SMEM, spec((2, head, tl), lambda i: (0, 0, i)), first_rows, second_rows, pair_rows, pair_rows,
                  pair_rows,
                  spec((16, tl), lambda i: (0, i)), cols2, rows, rows, rows, fixed((1, width)),
                  fixed((experts * head, width)), fixed((width, 2 * head)), fixed((2 * experts, width))],
        out_specs=[rows] + [fixed((share + 48, width))] * 4,
        out_shape=[shape((tokens, width), F32)] + [shape((share + 48, width), BF)] * 4,
        scratch_shapes=[
            pltpu.VMEM((experts * head, width), F32), pltpu.VMEM((2 * head, width), F32),
            pltpu.VMEM((8, width), F32),
        ],
        compiler_params=PARAMS,
        cost_estimate=cost(10),
    )(owners, q_grad, key0a, key0b, key_from1, key_from2, key_from3, logit, routes_t, normed, x, mid_grad, gain1, wq,
      shared_proj, router_t)

    near, far = group_sum(last)
    mine, total = lax.optimization_barrier((summed(near, far), total))
    total = total.astype(F32)
    ends = jnp.broadcast_to(mine[share:][None], (dp, 48, width))
    each = jnp.concatenate([by_holder(mine[:share]), ends], axis=1)
    got = lax.all_to_all(each, "dp", split_axis=0, concat_axis=0, tiled=True)
    got = jnp.sum(got.astype(F32), axis=0)
    wq_total = got[: share // dp].reshape(head // 4, -1)
    ends = got[share // dp :]
    block = width // 4
    each = 2 * head // 4
    shared_total = jnp.concatenate(
        [ends[:each, g * block : (g + 1) * block] for g in range(4)], axis=0
    )
    cut = lax.dynamic_slice_in_dim(total[2 * width : 2 * width + 16], me * block, block, axis=1)
    return (
        block_out.reshape(1, tokens, width),
        input_grad.reshape(1, tokens, width),
        ends[each, :block],
        ends[each + 1, :block],
        cut[8 : 8 + experts].T,
        shared_total.T,
        wq_total,
        wo_total,
        cut[1],
        cut[2],
        total[:width],
        total[2 * width + 3],
        total[width : 2 * width].T,
        cut[0],
    )


def solution(mesh):
    both = P("dp", "mp", None)
    table = P("mp", "dp")
    placed = (
        both, both, P("dp"), P(), P(), P(), P(), table, table, P(), P(), P(None, "mp"), P("mp"),
        P("mp", None), P(), both,
    )
    given = (
        both, both, P("mp"), P("mp"), P("mp", None), P("mp", None), table, table, P("mp"), P("mp"),
        P(None, "mp"), P("mp"), P("mp", None), P("mp"),
    )
    return jax.shard_map(on_device, mesh=mesh, in_specs=placed, out_specs=given, check_vma=False)
```

profile of v0, /device:TPU:0, one launch (start us, length us, event | category | flops | bytes accessed | tf_op | source)
XLA Modules:
  0.0 278.0 jit_solution(15725300279683957164)
XLA Ops:
  2.1 7.3 %all-to-all-start = ((bf16[8,32,512]{2,1,0:T(8,128)(2,1)}), bf16[8,32,512]{2,1,0:T(8,128)(2,1)S(1)}, u32[]{:S(2)}, u32[]{:S(2)}) async-start(bf16[8,32,512]{2,1,0:T(8,128)(2,1)} %broadcast_in_dim.18), calls=%async_computation | async-start | bytes 524288 | tf_op jit(solution)/shard_map/all_to_all | solution.py:398
  9.4 1.3 concatenate.18.router
  10.7 5.3 %shard_map.263 = (bf16[2048,512]{1,0:T(8,128)(2,1)}, bf16[2048,128]{1,0:T(8,128)(2,1)}, f32[2,2048]{1,0:T(2,128)}) custom-call(bf16[2048,512]{1,0:T(8,128)(2,1)} %bitcast.58, f32[1,512]{1,0:T(1,128)} %bitcast.68, f32[1,512]{1,0:T(1,128)} %bitcast.65, bf16[16,512]{1,0:T(8,128)(2,1)} %concatenate.18.router, bf16[512,128]{1,0:T(8,128)(2,1)} %proj.3, ...), custom_call_target="tpu_custom_call" | custom-call | flops 5500000256 | bytes 1024 | tf_op jit(solution)/shard_map/pallas_call | solution.py:448
  16.0 1.5 collective-permute-start.4
  20.8 10.2 %collective-permute-done.4.p2.rest_4_ = bf16[2048,128]{1,0:T(8,128)(2,1)S(1)} collective-permute-done((bf16[2048,128]{1,0:T(8,128)(2,1)}, bf16[2048,128]{1,0:T(8,128)(2,1)S(1)}, u32[]{:S(2)}, u32[]{:S(2)}) %collective-permute-start.4) | collective-permute-done | bytes 524320 | tf_op jit(solution)/shard_map/ppermute | solution.py:377
  31.6 1.5 collective-permute-start.7
  35.3 5.3 %shard_map.264 = (bf16[2,64,2048]{2,1,0:T(8,128)(2,1)}, bf16[2,2048,128]{2,1,0:T(8,128)(2,1)}, bf16[512,512]{1,0:T(8,128)(2,1)}) custom-call(s32[4]{0:T(128)} %iota_xor_fusion.where, bf16[2048,512]{1,0:T(8,128)(2,1)} %get-tuple-element.55.normed, bf16[128,512]{1,0:T(8,128)(2,1)} %bitcast.53, bf16[128,512]{1,0:T(8,128)(2,1)} %copy-done.17, ...), custom_call_target="tpu_custom_call" | custom-call | flops 5500000256 | bytes 1024 | tf_op jit(solution)/shard_map/pallas_call | solution.py:473
  41.6 34.6 %shard_map.265 = (f32[2,72,2048]{2,1,0:T(8,128)}, bf16[8192,4096]{1,0:T(8,128)(2,1)}) custom-call(s32[4]{0:T(128)} %subtract_clamp_fusion.live, bf16[2,64,2048]{2,1,0:T(8,128)(2,1)} %get-tuple-element.56.q, bf16[2048,128]{1,0:T(8,128)(2,1)} %get-tuple-element.57.p0.rest_5_.rest_4_, bf16[2048,128]{1,0:T(8,128)(2,1)} %copy-done.10, ...), custom_call_target="tpu_custom_call" | custom-call | flops 36300001280 | bytes 1024 | tf_op jit(solution)/shard_map/pallas_call | solution.py:486
  77.7 1.9 collective-permute-done.8.f3
  80.6 46.4 %shard_map.266 = (bf16[2048,512]{1,0:T(8,128)(2,1)}, f32[2048,512]{1,0:T(8,128)}, bf16[2,2048,128]{2,1,0:T(8,128)(2,1)}, bf16[2,128,2048]{2,1,0:T(8,128)(2,1)}, ...) custom-call(s32[4]{0:T(128)} %iota_xor_fusion.where, ...), custom_call_target="tpu_custom_call" | custom-call | flops 54999998464 | bytes 1024 | tf_op jit(solution)/shard_map/pallas_call | solution.py:513
  127.0 1.6 collective-permute-start.10
  129.2 47.4 %shard_map.267 = (f32[2,64,2048]{2,1,0:T(8,128)}, bf16[2048,128]{1,0:T(8,128)(2,1)}, bf16[2048,128]{1,0:T(8,128)(2,1)}, bf16[1024,128]{1,0:T(8,128)(2,1)}) custom-call(bf16[2,128,2048]{2,1,0:T(8,128)(2,1)} %get-tuple-element.64.dot, bf16[2,2048,128]{2,1,0:T(8,128)(2,1)} %get-tuple-element.65.do, bf16[2,2048,128]{2,1,0:T(8,128)(2,1)} %get-tuple-element.66.q, ...), custom_call_target="tpu_custom_call" | custom-call | flops 60500000768 | bytes 1024 | tf_op jit(solution)/shard_map/pallas_call | solution.py:542
  176.6 6.4 %collective-permute-done.9 = bf16[1216,512]{1,0:T(8,128)(2,1)S(1)} collective-permute-done((bf16[1216,512]{1,0:T(8,128)(2,1)}, bf16[1216,512]{1,0:T(8,128)(2,1)S(1)}, u32[]{:S(2)}, u32[]{:S(2)}) %collective-permute-start.9) | collective-permute-done | bytes 1245216 | tf_op jit(solution)/shard_map/ppermute | solution.py:377
  184.9 5.6 %all-to-all-start.1 = ((bf16[8,152,512]{2,1,0:T(8,128)(2,1)}), bf16[8,152,512]{2,1,0:T(8,128)(2,1)S(1)}, u32[]{:S(2)}, u32[]{:S(2)}) async-start(bf16[8,152,512]{2,1,0:T(8,128)(2,1)} %pad_maximum_fusion), calls=%async_computation.1 | async-start | bytes 2490368 | tf_op jit(solution)/shard_map/all_to_all | solution.py:574
  190.5 1.6 collective-permute-start.13
  192.1 29.5 %shard_map.268 = (f32[2,64,2048]{2,1,0:T(8,128)}, bf16[2048,128]{1,0:T(8,128)(2,1)}, bf16[1024,128]{1,0:T(8,128)(2,1)}) custom-call(bf16[2,128,2048]{2,1,0:T(8,128)(2,1)} %get-tuple-element.64.dot, bf16[2,2048,128]{2,1,0:T(8,128)(2,1)} %get-tuple-element.65.do, bf16[2,2048,128]{2,1,0:T(8,128)(2,1)} %get-tuple-element.66.q, ...), custom_call_target="tpu_custom_call", output_to_operand_aliasing={{0}: (3, {})} | custom-call | flops 38499999744 | bytes 1024 | tf_op jit(solution)/shard_map/pallas_call | solution.py:542
  223.6 5.9 %all-to-all-start.2 = ((bf16[8,136,512]{2,1,0:T(8,128)(2,1)}), bf16[8,136,512]{2,1,0:T(8,128)(2,1)S(1)}, u32[]{:S(2)}, u32[]{:S(2)}) async-start(bf16[8,136,512]{2,1,0:T(8,128)(2,1)} %broadcast_in_dim.44), calls=%async_computation.2 | async-start | bytes 2228224 | tf_op jit(solution)/shard_map/all_to_all | solution.py:398
  230.5 10.6 %shard_map.269 = (f32[2048,512]{1,0:T(8,128)}, bf16[176,512]{1,0:T(8,128)(2,1)}, bf16[176,512]{1,0:T(8,128)(2,1)}, bf16[176,512]{1,0:T(8,128)(2,1)}, bf16[176,512]{1,0:T(8,128)(2,1)}) custom-call(s32[4]{0:T(128)} %iota_xor_fusion.where, f32[2,64,2048]{2,1,0:T(8,128)} %get-tuple-element.79.dq, bf16[1024,128]{1,0:T(8,128)(2,1)} %get-tuple-element.80.pa, ...), custom_call_target="tpu_custom_call" | custom-call | flops 11000000512 | bytes 1024 | tf_op jit(solution)/shard_map/pallas_call | solution.py:589
  243.8 1.6 collective-permute-start.17
  245.4 5.0 %collective-permute-done.17 = bf16[176,512]{1,0:T(8,128)(2,1)S(1)} collective-permute-done((bf16[176,512]{1,0:T(8,128)(2,1)S(1)}, bf16[176,512]{1,0:T(8,128)(2,1)S(1)}, u32[]{:S(2)}, u32[]{:S(2)}) %collective-permute-start.17) | collective-permute-done | bytes 180256 | tf_op jit(solution)/shard_map/ppermute | solution.py:377
  251.4 5.4 %all-to-all-done.2 = bf16[8,136,512]{2,1,0:T(8,128)(2,1)S(1)} async-done(((bf16[8,136,512]{2,1,0:T(8,128)(2,1)}), bf16[8,136,512]{2,1,0:T(8,128)(2,1)S(1)}, u32[]{:S(2)}, u32[]{:S(2)}) %all-to-all-start.2) | async-done | bytes 1114144 | tf_op jit(solution)/shard_map/all_to_all | solution.py:398
  257.8 3.6 %all-to-all-start.3 = ((bf16[8,64,512]{2,1,0:T(8,128)(2,1)}), bf16[8,64,512]{2,1,0:T(8,128)(2,1)S(1)}, u32[]{:S(2)}, u32[]{:S(2)}) async-start(bf16[8,64,512]{2,1,0:T(8,128)(2,1)} %pad_maximum_fusion.2), calls=%async_computation.3 | async-start | bytes 1048576 | tf_op jit(solution)/shard_map/all_to_all | solution.py:612
  264.1 1.3 copy.38
  266.6 9.5 %all-to-all-done.3 = bf16[8,64,512]{2,1,0:T(8,128)(2,1)S(1)} async-done(((bf16[8,64,512]{2,1,0:T(8,128)(2,1)}), bf16[8,64,512]{2,1,0:T(8,128)(2,1)S(1)}, u32[]{:S(2)}, u32[]{:S(2)}) %all-to-all-start.3) | async-done | bytes 524320 | tf_op jit(solution)/shard_map/all_to_all | solution.py:612
  (104 shorter events, 26.0 us)
Async XLA Ops:
  2.1 16.5 %all-to-all-start = ((bf16[8,32,512]{2,1,0:T(8,128)(2,1)}), bf16[8,32,512]{2,1,0:T(8,128)(2,1)S(1)}, u32[]{:S(2)}, u32[]{:S(2)}) async-start(bf16[8,32,512]{2,1,0:T(8,128)(2,1)} %broadcast_in_dim.18), calls=%async_computation | async-start | bytes 524288 | tf_op jit(solution)/shard_map/all_to_all | solution.py:398
  16.0 15.1 %collective-permute-start.4 = (bf16[2048,128]{1,0:T(8,128)(2,1)}, bf16[2048,128]{1,0:T(8,128)(2,1)S(1)}, u32[]{:S(2)}, u32[]{:S(2)}) collective-permute-start(bf16[2048,128]{1,0:T(8,128)(2,1)} %get-tuple-element.57.p0.rest_5_.rest_4_), channel_id=1, source_target_pairs={{0,2},{1,3},{2,0},{3,1},{4,6},{5,7},{6,4},{7,5},{8,10},{9,11},{10,... | collective-permute-start | bytes 1572872 | tf_op jit(solution)/shard_map/ppermute | solution.py:377
  17.5 23.1 %collective-permute-start.3 = (bf16[2048,128]{1,0:T(8,128)(2,1)}, bf16[2048,128]{1,0:T(8,128)(2,1)S(1)}, u32[]{:S(2)}, u32[]{:S(2)}) collective-permute-start(bf16[2048,128]{1,0:T(8,128)(2,1)} %get-tuple-element.57.p0.rest_5_.rest_4_), channel_id=1, source_target_pairs={{0,1},{1,0},{2,3},{3,2},{4,5},{5,4},{6,7},{7,6},{8,9},{9,8},{10,11... | collective-permute-start | bytes 1572872 | tf_op jit(solution)/shard_map/ppermute | solution.py:377
  18.7 12.9 %collective-permute-start = (bf16[128,512]{1,0:T(8,128)(2,1)S(1)}, bf16[128,512]{1,0:T(8,128)(2,1)S(1)}, u32[]{:S(2)}, u32[]{:S(2)}) collective-permute-start(bf16[128,512]{1,0:T(8,128)(2,1)S(1)} %bitcast.50), channel_id=1, source_target_pairs={{0,1},{1,0},{2,3},{3,2},{4,5},{5,4},{6,7},{7,6},{8,9},{9,8},{10,11... | collective-permute-start | bytes 393224 | tf_op jit(solution)/shard_map/ppermute | solution.py:377
  19.3 14.5 %collective-permute-start.1 = (bf16[128,512]{1,0:T(8,128)(2,1)S(1)}, bf16[128,512]{1,0:T(8,128)(2,1)S(1)}, u32[]{:S(2)}, u32[]{:S(2)}) collective-permute-start(bf16[128,512]{1,0:T(8,128)(2,1)S(1)} %bitcast.51), channel_id=1, source_target_pairs={{0,2},{1,3},{2,0},{3,1},{4,6},{5,7},{6,4},{7,5},{8,10},{9,11},{10,... | collective-permute-start | bytes 393224 | tf_op jit(solution)/shard_map/ppermute | solution.py:377
  20.0 14.7 %collective-permute-start.2 = (bf16[128,512]{1,0:T(8,128)(2,1)S(1)}, bf16[128,512]{1,0:T(8,128)(2,1)S(1)}, u32[]{:S(2)}, u32[]{:S(2)}) collective-permute-start(bf16[128,512]{1,0:T(8,128)(2,1)S(1)} %bitcast.52), channel_id=1, source_target_pairs={{0,3},{1,2},{2,1},{3,0},{4,7},{5,6},{6,5},{7,4},{8,11},{9,10},{10,... | collective-permute-start | bytes 393224 | tf_op jit(solution)/shard_map/ppermute | solution.py:377
  31.0 9.6 %collective-permute-start.5 = (bf16[2048,128]{1,0:T(8,128)(2,1)S(1)}, bf16[2048,128]{1,0:T(8,128)(2,1)S(1)}, u32[]{:S(2)}, u32[]{:S(2)}) collective-permute-start(bf16[2048,128]{1,0:T(8,128)(2,1)S(1)} %collective-permute-done.4.p2.rest_4_), channel_id=1, source_target_pairs={{0,1},{1,0},{2,3},{3,2},{4,5},{5,4},{6,7},{7,6},{8,9},{9,8},{10,11... | collective-permute-start | bytes 1572872 | tf_op jit(solution)/shard_map/ppermute | solution.py:377
  31.6 44.6 %collective-permute-start.7 = (bf16[1168,512]{1,0:T(8,128)(2,1)S(1)}, bf16[1168,512]{1,0:T(8,128)(2,1)S(1)}, u32[]{:S(2)}, u32[]{:S(2)}) collective-permute-start(bf16[1168,512]{1,0:T(8,128)(2,1)S(1)} %pad_maximum_fusion.1.f0), channel_id=1, source_target_pairs={{0,2},{1,3},{2,0},{3,1},{4,6},{5,7},{6,4},{7,5},{8,10},{9,11},{10,... | collective-permute-start | bytes 3588104 | tf_op jit(solution)/shard_map/ppermute | solution.py:377
  33.8 43.9 %collective-permute-start.6 = (bf16[1168,512]{1,0:T(8,128)(2,1)S(1)}, bf16[1168,512]{1,0:T(8,128)(2,1)S(1)}, u32[]{:S(2)}, u32[]{:S(2)}) collective-permute-start(bf16[1168,512]{1,0:T(8,128)(2,1)S(1)} %pad_maximum_fusion.1.f0), channel_id=1, source_target_pairs={{0,1},{1,0},{2,3},{3,2},{4,5},{5,4},{6,7},{7,6},{8,9},{9,8},{10,11... | collective-permute-start | bytes 3588104 | tf_op jit(solution)/shard_map/ppermute | solution.py:377
  41.6 35.5 %copy-start.6 = (bf16[512]{0:T(512)(128)(2,1)S(1)}, bf16[512]{0:T(512)(128)(2,1)}, u32[]{:S(2)}) copy-start(bf16[512]{0:T(512)(128)(2,1)} %param.30) | copy-start | bytes 3076
  76.2 3.4 %collective-permute-start.8 = (bf16[1168,512]{1,0:T(8,128)(2,1)S(1)}, bf16[1168,512]{1,0:T(8,128)(2,1)S(1)}, u32[]{:S(2)}, u32[]{:S(2)}) collective-permute-start(bf16[1168,512]{1,0:T(8,128)(2,1)S(1)} %collective-permute-done.7.f2), channel_id=1, source_target_pairs={{0,1},{1,0},{2,3},{3,2},{4,5},{5,4},{6,7},{7,6},{8,9},{9,8},{10,11... | collective-permute-start | bytes 3588104 | tf_op jit(solution)/shard_map/ppermute | solution.py:377
  127.0 49.6 %collective-permute-start.10 = (bf16[1216,512]{1,0:T(8,128)(2,1)}, bf16[1216,512]{1,0:T(8,128)(2,1)S(1)}, u32[]{:S(2)}, u32[]{:S(2)}) collective-permute-start(bf16[1216,512]{1,0:T(8,128)(2,1)} %get-tuple-element.71), channel_id=1, source_target_pairs={{0,2},{1,3},{2,0},{3,1},{4,6},{5,7},{6,4},{7,5},{8,10},{9,11},{10,... | collective-permute-start | bytes 3735560 | tf_op jit(solution)/shard_map/ppermute | solution.py:377
  128.6 48.0 %collective-permute-start.11 = (bf16[1216,512]{1,0:T(8,128)(2,1)}, bf16[1216,512]{1,0:T(8,128)(2,1)S(1)}, u32[]{:S(2)}, u32[]{:S(2)}) collective-permute-start(bf16[1216,512]{1,0:T(8,128)(2,1)} %get-tuple-element.72), channel_id=1, source_target_pairs={{0,1},{1,0},{2,3},{3,2},{4,5},{5,4},{6,7},{7,6},{8,9},{9,8},{10,11... | collective-permute-start | bytes 3735560 | tf_op jit(solution)/shard_map/ppermute | solution.py:377
  128.7 54.4 %collective-permute-start.9 = (bf16[1216,512]{1,0:T(8,128)(2,1)}, bf16[1216,512]{1,0:T(8,128)(2,1)S(1)}, u32[]{:S(2)}, u32[]{:S(2)}) collective-permute-start(bf16[1216,512]{1,0:T(8,128)(2,1)} %get-tuple-element.70), channel_id=1, source_target_pairs={{0,3},{1,2},{2,1},{3,0},{4,7},{5,6},{6,5},{7,4},{8,11},{9,10},{10,... | collective-permute-start | bytes 3735560 | tf_op jit(solution)/shard_map/ppermute | solution.py:377
  129.2 53.8 %copy-start = (bf16[1216,512]{1,0:T(8,128)(2,1)S(1)}, bf16[1216,512]{1,0:T(8,128)(2,1)}, u32[]{:S(2)}) copy-start(bf16[1216,512]{1,0:T(8,128)(2,1)} %get-tuple-element.69) | copy-start | bytes 3735556
  184.9 36.7 %all-to-all-start.1 = ((bf16[8,152,512]{2,1,0:T(8,128)(2,1)}), bf16[8,152,512]{2,1,0:T(8,128)(2,1)S(1)}, u32[]{:S(2)}, u32[]{:S(2)}) async-start(bf16[8,152,512]{2,1,0:T(8,128)(2,1)} %pad_maximum_fusion), calls=%async_computation.1 | async-start | bytes 2490368 | tf_op jit(solution)/shard_map/all_to_all | solution.py:574
  190.5 39.0 %collective-permute-start.13 = (bf16[2048,128]{1,0:T(8,128)(2,1)S(1)}, bf16[2048,128]{1,0:T(8,128)(2,1)S(1)}, u32[]{:S(2)}, u32[]{:S(2)}) collective-permute-start(bf16[2048,128]{1,0:T(8,128)(2,1)S(1)} %copy-done.14), channel_id=1, source_target_pairs={{0,2},{1,3},{2,0},{3,1},{4,6},{5,7},{6,4},{7,5},{8,10},{9,11},{10,... | collective-permute-start | bytes 1572872 | tf_op jit(solution)/shard_map/ppermute | solution.py:377
  192.1 37.4 %collective-permute-start.14 = (bf16[2048,128]{1,0:T(8,128)(2,1)S(1)}, bf16[2048,128]{1,0:T(8,128)(2,1)}, u32[]{:S(2)}, u32[]{:S(2)}) collective-permute-start(bf16[2048,128]{1,0:T(8,128)(2,1)S(1)} %copy-done.13), channel_id=1, source_target_pairs={{0,3},{1,2},{2,1},{3,0},{4,7},{5,6},{6,5},{7,4},{8,11},{9,10},{10,... | collective-permute-start | bytes 1572872 | tf_op jit(solution)/shard_map/ppermute | solution.py:377
  221.8 7.7 %collective-permute-start.12 = (bf16[2048,128]{1,0:T(8,128)(2,1)}, bf16[2048,128]{1,0:T(8,128)(2,1)S(1)}, u32[]{:S(2)}, u32[]{:S(2)}) collective-permute-start(bf16[2048,128]{1,0:T(8,128)(2,1)} %get-tuple-element.82), channel_id=1, source_target_pairs={{0,1},{1,0},{2,3},{3,2},{4,5},{5,4},{6,7},{7,6},{8,9},{9,8},{10,11... | collective-permute-start | bytes 1572872 | tf_op jit(solution)/shard_map/ppermute | solution.py:377
  223.6 33.3 %all-to-all-start.2 = ((bf16[8,136,512]{2,1,0:T(8,128)(2,1)}), bf16[8,136,512]{2,1,0:T(8,128)(2,1)S(1)}, u32[]{:S(2)}, u32[]{:S(2)}) async-start(bf16[8,136,512]{2,1,0:T(8,128)(2,1)} %broadcast_in_dim.44), calls=%async_computation.2 | async-start | bytes 2228224 | tf_op jit(solution)/shard_map/all_to_all | solution.py:398
  241.1 1.7 collective-permute-start.16
  241.2 4.2 %collective-permute-start.15 = (bf16[176,512]{1,0:T(8,128)(2,1)}, bf16[176,512]{1,0:T(8,128)(2,1)S(1)}, u32[]{:S(2)}, u32[]{:S(2)}) collective-permute-start(bf16[176,512]{1,0:T(8,128)(2,1)} %get-tuple-element.90), channel_id=1, source_target_pairs={{0,1},{1,0},{2,3},{3,2},{4,5},{5,4},{6,7},{7,6},{8,9},{9,8},{10,11... | collective-permute-start | bytes 540680 | tf_op jit(solution)/shard_map/ppermute | solution.py:377
  243.8 6.7 %collective-permute-start.17 = (bf16[176,512]{1,0:T(8,128)(2,1)S(1)}, bf16[176,512]{1,0:T(8,128)(2,1)S(1)}, u32[]{:S(2)}, u32[]{:S(2)}) collective-permute-start(bf16[176,512]{1,0:T(8,128)(2,1)S(1)} %add_convert_fusion.2), channel_id=1, source_target_pairs={{0,2},{1,3},{2,0},{3,1},{4,6},{5,7},{6,4},{7,5},{8,10},{9,11},{10,... | collective-permute-start | bytes 540680 | tf_op jit(solution)/shard_map/ppermute | solution.py:377
  257.8 18.3 %all-to-all-start.3 = ((bf16[8,64,512]{2,1,0:T(8,128)(2,1)}), bf16[8,64,512]{2,1,0:T(8,128)(2,1)S(1)}, u32[]{:S(2)}, u32[]{:S(2)}) async-start(bf16[8,64,512]{2,1,0:T(8,128)(2,1)} %pad_maximum_fusion.2), calls=%async_computation.3 | async-start | bytes 1048576 | tf_op jit(solution)/shard_map/all_to_all | solution.py:612
  (18 other events, 102.6 us)
where the time goes:
time: 279 us; the launch traced here: 278 us
  Pallas kernels  179 us (64%)
  waiting for transfers between devices  41.2 us (15%)
  starting transfers between devices  34.9 us (13%)
  local copies, waits for them, and re-layouts  13.6 us (5%)
  other arithmetic  7.59 us (3%)
    pallas_call x2, Pallas kernels, back_call(): pl.pallas_call(functools.partial(attend_back_kernel, head=head, places=pl...  76.9 us
    pallas_call x1, Pallas kernels, on_device(): pl.pallas_call(functools.partial(middle_kernel, head=head, experts=expert...  46.4 us
    pallas_call x1, Pallas kernels, on_device(): pl.pallas_call(functools.partial(attend_kernel, head=head, span=4 * token...  34.6 us
    ppermute x18, waiting for transfers between devices, swapped(): return lax.ppermute(value, 'mp', [(i, i ^ bit) for i in range(4)])  26.2 us
    all_to_all x2, starting transfers between devices, sent_to_all(): return lax.all_to_all(wide, axes, split_axis=0, concat_axis=0, tiled=True)  13.2 us
    ppermute x18, starting transfers between devices, swapped(): return lax.ppermute(value, 'mp', [(i, i ^ bit) for i in range(4)])  12.5 us
    pallas_call x1, Pallas kernels, on_device(): pl.pallas_call(functools.partial(last_kernel, head=head, experts=experts,...  10.6 us
    all_to_all x1, waiting for transfers between devices, on_device(): got = lax.all_to_all(each, 'dp', split_axis=0, concat_axis=0, tiled=True)  9.49 us
  transfers between devices with their start and end apart: 22, of which 9 were waited for; matrix products, arithmetic and copies ran while one was open for 4% of the time, Pallas kernels for 48%

commit v1 on v0

--- a/solution.py
+++ b/solution.py
@@ -111,6 +111,14 @@
     gates[1:2, :] = up1 * inverse
 
 
+def query_kernel(normed, table, routes, queries, q_rows, *, experts, scale):
+    every = nt(table[...], normed[...]) * scale
+    for s in range(2):
+        one = picked(every, routes[s : s + 1, :], experts)
+        queries[s] = one.astype(BF)
+        q_rows[s] = jnp.concatenate([one, jnp.zeros_like(one)], axis=0).T.astype(BF)
+
+
 def assembled(table, shares, where, experts, start):
     head = table.shape[0] // experts
     share = head // 4
@@ -121,19 +129,7 @@
             table[pl.ds(at, share), :] = part[here, :]
 
 
-def query_kernel(where, normed, t0, t1, t2, t3, routes, queries, q_rows, table, *, experts, scale):
-    @pl.when(pl.program_id(0) == 0)
-    def _():
-        assembled(table, (t0, t1, t2, t3), where, experts, 0)
-
-    every = nt(table[...], normed[...]) * scale
-    for s in range(2):
-        one = picked(every, routes[s : s + 1, :], experts)
-        queries[s] = one.astype(BF)
-        q_rows[s] = jnp.concatenate([one, jnp.zeros_like(one)], axis=0).T.astype(BF)
-
-
-def attend_kernel(live, q, p0, p1, p2, p3, out, kept, keys, values, limit, top, *, head, span):
+def attend_kernel(where, length, q, p0, p1, p2, p3, out, kept, keys, values, limit, top, *, head, span):
     part = p0.shape[0]
 
     @pl.when((pl.program_id(0) == 0) & (pl.program_id(1) == 0))
@@ -145,7 +141,8 @@
         longest = jnp.zeros((1, LANES), F32)
         for o, p in enumerate((p0, p1, p2, p3)):
             pair = p[...]
-            keys[o * part : (o + 1) * part, :] = key_rows(pair, live[o], head)
+            live = length[0] - where[o] * part
+            keys[o * part : (o + 1) * part, :] = key_rows(pair, live, head)
             turned = nt(move, pair)
             line = lax.broadcasted_iota(jnp.int32, turned.shape, 0)
             values[:, o * part : (o + 1) * part] = jnp.where(line == head, 1.0, turned).astype(BF)
@@ -188,9 +185,11 @@
     out[0, head : head + 8, :] = jnp.broadcast_to(inverse, (8, n))
 
 
-def attend_back_kernel(dot, do, q, *rest, head, places, first):
+def attend_back_kernel(dot, do, q, *rest, head, places, first, carry):
     if not first:
         before, *rest = rest
+    if carry:
+        carried, *rest = rest
     pieces = len(places)
     weights, pairs, after = rest[:pieces], rest[pieces : 2 * pieces], rest[2 * pieces]
     grads = rest[2 * pieces + 1 : 3 * pieces + 1]
@@ -223,15 +222,20 @@
 
     @pl.when(step == pl.num_programs(0) - 1)
     def _():
-        for grad, here in zip(grads, spans):
-            lane = lax.broadcasted_iota(jnp.int32, grad.shape, 1)
-            grad[...] = (both[here, :] * jnp.where(lane < head, LN2, 1.0)).astype(BF)
+        for n, (grad, here) in enumerate(zip(grads, spans)):
+            at = 0
+            if carry and n == 0:
+                at = carried.shape[0]
+                grad[0:at, :] = carried[...]
+            size = sizes[n]
+            lane = lax.broadcasted_iota(jnp.int32, (size, LANES), 1)
+            grad[at : at + size, :] = (both[here, :] * jnp.where(lane < head, LN2, 1.0)).astype(BF)
 
 
 def middle_kernel(
     where, att, routes, gates, x, up, normed,
-    f0, f1, f2, f3, rb, gain, bias,
-    out, mid_grad, do_rows, do_t, logit, g0, g1, g2, g3,
+    f0, f1, f2, f3, gain, bias,
+    active, kept, mid_grad, do_rows, do_t, logit, g0, g1, g2, g3,
     we_sum, wr_sum, wo_sum, eb_sum, small, rt_sum, wo,
     *, head, experts,
 ):
@@ -256,29 +260,30 @@
     upt = upstream.T
     ff = f0.shape[1]
     width = middle.shape[1]
-    reduced = jnp.zeros(middle.shape, F32)
     two_grad = jnp.zeros(middle.shape, F32)
+    backs = []
     for o, f in enumerate((f0, f1, f2, f3)):
         here = slice(o * ff, (o + 1) * ff)
-        we, wr = f[0:width, :], f[width : width + ff, :]
-        v = nn(normed_two, we) + f[width + ff : width + ff + 16, :].astype(F32)[0:1, :]
+        v = nn(normed_two, f[0:width, :])
+        v = v + f[width + ff : width + ff + 16, :].astype(F32)[0:1, :]
         square = v * v
         inner = v * (GELU_A + (GELU_A * GELU_B) * square)
         half = 0.5 + 0.5 * jnp.tanh(inner)
         act = v * half
-        slope = half + 2.0 * act * (1.0 - half) * (GELU_A + (3.0 * GELU_A * GELU_B) * square)
-        low = act.astype(BF)
-        reduced = reduced + nn(low, wr)
-        back = nt(upstream, wr) * slope
-        back_low = back.astype(BF)
-        two_grad = two_grad + nt(back_low, we)
-        we_sum[:, here] += nn(n2t, back_low)
-        wr_sum[:, here] += nn(upt, low)
-        eb_sum[0:1, here] += jnp.sum(back_low.astype(F32), axis=0, keepdims=True)
-    out[...] = (middle + reduced + rb[...]).astype(BF)
+        slope = half + act * (1.0 - half) * (2.0 * GELU_A + (6.0 * GELU_A * GELU_B) * square)
+        active[:, here] = act.astype(BF)
+        backs.append((nt(upstream, f[width : width + ff, :]) * slope).astype(BF))
+    for o, f in enumerate((f0, f1, f2, f3)):
+        here = slice(o * ff, (o + 1) * ff)
+        back = backs[o]
+        two_grad = two_grad + nt(back, f[0:width, :])
+        we_sum[:, here] += nn(n2t, back)
+        wr_sum[:, here] += nn(upt, active[:, here])
+        eb_sum[0:1, here] += jnp.sum(back.astype(F32), axis=0, keepdims=True)
+    kept[...] = middle.astype(BF)
     wide_up = upstream.astype(F32)
     mid = wide_up + norm_back(two_grad, normal, inverse, gain[...])
-    mid_grad[...] = mid
+    mid_grad[...] = mid.astype(BF)
     small[0:1, :] += jnp.sum(wide_up, axis=0, keepdims=True)
     small[1:2, :] += jnp.sum(two_grad * normal, axis=0, keepdims=True)
     small[2:3, :] += jnp.sum(two_grad, axis=0, keepdims=True)
@@ -327,7 +332,7 @@
 
 
 def last_kernel(
-    where, dq, pa, pd, p1, p2, p3, logit, routes, normed, x, mid_grad, gain, wq, proj, router,
+    where, dq, p0, p1, p2, p3, logit, routes, normed, x, wq, proj, router,
     out, s0, s1, s2, s3, wq_sum, sp_sum, small, *, head, experts, scale,
 ):
     step = pl.program_id(0)
@@ -340,7 +345,7 @@
     route0, route1 = routes[0:1, :], routes[1:2, :]
     grad0, grad1 = dq[0] * scale, dq[1] * scale
     placed = spread(grad0, grad1, route0, route1, experts).astype(BF)
-    own = jnp.where(step < pl.num_programs(0) // 2, pa[...].astype(F32), pd[...].astype(F32))
+    own = p0[...].astype(F32)
     for p in (p1, p2, p3):
         own = own + p[...].astype(F32)
     pair = own.astype(BF)
@@ -348,8 +353,8 @@
     here_normed = normed[...]
     wq_sum[...] += nn(placed, here_normed)
     sp_sum[...] += tn(pair, here_normed)
-    normal, inverse = norm_parts(x[...].astype(F32))
-    out[...] = mid_grad[...] + norm_back(normed_grad, normal, inverse, gain[...])
+    normal, _ = norm_parts(x[...].astype(F32))
+    out[...] = normed_grad.astype(BF)
     small[0:1, :] += jnp.sum(normed_grad * normal, axis=0, keepdims=True)
     small[1:2, :] += jnp.sum(normed_grad, axis=0, keepdims=True)
 
@@ -366,13 +371,26 @@
                 s[e * share : (e + 1) * share, :] = wq_sum[pl.ds(at, share), :].astype(BF)
             lanes = pl.ds(pl.multiple_of(owner * block, block), block)
             s[table + each : table + each + 16, :] = jnp.zeros((16, 4 * block), BF)
-            ends = jnp.concatenate([small[:, lanes], jnp.zeros((8, block), F32)], axis=0)
-            s[table + each : table + each + 16, 0:block] = ends.astype(BF)
+            line = lax.broadcasted_iota(jnp.int32, (16, block), 0)
+            for g in range(2):
+                ends = jnp.where(line == 0, small[g : g + 1, lanes], 0.0)
+                s[table + each : table + each + 16, g * block : (g + 1) * block] = ends.astype(BF)
             for g in range(4):
                 piece = sp_sum[g * each : (g + 1) * each, lanes]
                 s[table : table + each, g * block : (g + 1) * block] = piece.astype(BF)
 
 
+def outputs_kernel(active, middle, r0, r1, r2, r3, rb, normed_grad, x, mid_grad, gain, out, x_grad):
+    ff = r0.shape[0]
+    total = middle[...].astype(F32) + rb[...]
+    for o, r in enumerate((r0, r1, r2, r3)):
+        total = total + nn(active[:, o * ff : (o + 1) * ff], r[...])
+    out[...] = total.astype(BF)
+    normal, inverse = norm_parts(x[...].astype(F32))
+    back = norm_back(normed_grad[...].astype(F32), normal, inverse, gain[...])
+    x_grad[...] = mid_grad[...].astype(F32) + back
+
+
 def swapped(value, bit):
     return lax.ppermute(value, "mp", [(i, i ^ bit) for i in range(4)])
 
@@ -384,18 +402,20 @@
 
 def summed(a, b):
     return (a.astype(F32) + b.astype(F32)).astype(BF)
-
-
-def group_sum(parts):
-    far = summed(parts[2], swapped(parts[3], 1))
-    near = summed(parts[0], swapped(parts[1], 1))
-    return near, swapped(far, 2)
 
 
 def sent_to_all(value, axes):
     n = lax.axis_size(axes)
     wide = jnp.broadcast_to(value[None], (n,) + value.shape)
     return lax.all_to_all(wide, axes, split_axis=0, concat_axis=0, tiled=True)
+
+
+def whole_table(share, experts):
+    dp, mp = lax.axis_size("dp"), lax.axis_size("mp")
+    rows, cols = share.shape
+    every = sent_to_all(share, ("dp", "mp"))
+    each = every.reshape(experts, dp // experts, mp, rows, cols)
+    return each.transpose(0, 2, 3, 1, 4).reshape(experts * mp * rows, dp // experts * cols)
 
 
 def spec(shape, index):
@@ -434,13 +454,14 @@
     units = expand_weight.shape[1]
     me = lax.axis_index("mp")
     owners = me ^ jnp.arange(4, dtype=jnp.int32)
-    live = jnp.clip(lengths[0] - owners * tokens, 0, tokens)
     x = block_input.reshape(tokens, width)
     up = upstream_grad.reshape(tokens, width)
     routes_t = routes.reshape(tokens, 2).T
-    router_t = jnp.concatenate([router_weight.T, jnp.zeros((experts, width), BF)], axis=0)
+    router_t = jnp.pad(router_weight.T, ((0, experts), (0, 0)))
     gain1, bias1 = first_gain[None], first_bias[None]
     gain2, bias2 = second_gain[None], second_bias[None]
+
+    wq = whole_table(query_weight, experts)
 
     tb = 512
     rows = spec((tb, width), lambda i: (i, 0))
@@ -458,35 +479,32 @@
 
     pair_across = swapped(pairs, 2)
     pair_beside = swapped(pairs, 1)
-    both = jnp.concatenate([query_weight, output_weight], axis=0)
-    shares = sent_to_all(both, "dp")
-    shares = shares.reshape(experts, dp // experts, 2, head // 4, -1).transpose(2, 0, 3, 1, 4)
-    shares = shares.reshape(2, experts * head // 4, width)
-    table = [shares[0]] + [swapped(shares[0], bit) for bit in (1, 2, 3)]
+    output_weight, wq = lax.optimization_barrier((output_weight, wq))
+    o_share = sent_to_all(output_weight, "dp")
+    o_share = o_share.reshape(experts, dp // experts, head // 4, -1).transpose(0, 2, 1, 3)
+    o_share = o_share.reshape(experts * head // 4, width)
+    queries, q_rows = pl.pallas_call(
+        functools.partial(query_kernel, experts=experts, scale=0.125 * LOG2E),
+        grid=(tokens // tb,),
+        in_specs=[rows, fixed((experts * head, width)), cols2],
+        out_specs=[spec((2, head, tb), lambda i: (0, 0, i)), spec((2, tb, LANES), lambda i: (0, i, 0))],
+        out_shape=[shape((2, head, tokens), BF), shape((2, tokens, LANES), BF)],
+        compiler_params=PARAMS,
+        cost_estimate=cost(5),
+    )(normed, wq, routes_t)
     feed = jnp.concatenate(
-        [expand_weight, reduce_weight, jnp.broadcast_to(expand_bias[None], (16, units)), shares[1]],
+        [expand_weight, reduce_weight, jnp.broadcast_to(expand_bias[None], (16, units)), o_share],
         axis=0,
     )
-    feed, pair_across = lax.optimization_barrier((feed, pair_across))
+    feed, pair_across, queries = lax.optimization_barrier((feed, pair_across, queries))
     pair = (pairs, pair_beside, pair_across, swapped(pair_across, 1))
     feed_across = swapped(feed, 2)
-    queries, q_rows, wq = pl.pallas_call(
-        functools.partial(query_kernel, experts=experts, scale=0.125 * LOG2E),
-        grid=(tokens // tb,),
-        in_specs=[SMEM, rows] + [fixed((experts * head // 4, width))] * 4 + [cols2],
-        out_specs=[spec((2, head, tb), lambda i: (0, 0, i)), spec((2, tb, LANES), lambda i: (0, i, 0)),
-                   fixed((experts * head, width))],
-        out_shape=[shape((2, head, tokens), BF), shape((2, tokens, LANES), BF),
-                   shape((experts * head, width), BF)],
-        compiler_params=PARAMS,
-        cost_estimate=cost(5),
-    )(owners, normed, *table, routes_t)
 
     tq = 512
     att, kept = pl.pallas_call(
         functools.partial(attend_kernel, head=head, span=4 * tokens),
         grid=(2, tokens // tq),
-        in_specs=[SMEM, spec((1, head, tq), lambda s, i: (s, 0, i))] + [fixed((tokens, 2 * head))] * 4,
+        in_specs=[SMEM, SMEM, spec((1, head, tq), lambda s, i: (s, 0, i))] + [fixed((tokens, 2 * head))] * 4,
         out_specs=[spec((1, head + 8, tq), lambda s, i: (s, 0, i)),
                    spec((4 * tokens, tq), lambda s, i: (0, s * (tokens // tq) + i))],
         out_shape=[shape((2, head + 8, tokens), F32), shape((4 * tokens, 2 * tokens), BF)],
@@ -496,7 +514,7 @@
         ],
         compiler_params=PARAMS,
         cost_estimate=cost(33),
-    )(live, queries, *pair)
+    )(owners, lengths, queries, *pair)
 
     feed_across = tied(feed_across, att)
     feeds = (feed, swapped(feed, 1), feed_across, swapped(feed_across, 1))
@@ -510,15 +528,15 @@
     both_rows = spec((2, tm, LANES), lambda i: (0, i, 0))
     both_cols = spec((2, LANES, tm), lambda i: (0, 0, i))
     att_cols = spec((2, head + 8, tm), lambda i: (0, 0, i))
-    block_out, mid_grad, do_rows, do_t, logit, *ffn = pl.pallas_call(
+    active, middle, mid_grad, do_rows, do_t, logit, *ffn = pl.pallas_call(
         functools.partial(middle_kernel, head=head, experts=experts),
         grid=(tokens // tm,),
         in_specs=[SMEM, att_cols, cols2, cols2, rows, rows, rows]
-        + [fixed(feed.shape)] * 4 + [fixed((1, width))] * 3,
-        out_specs=[rows, rows, both_rows, both_cols, spec((16, tm), lambda i: (0, i))]
+        + [fixed(feed.shape)] * 4 + [fixed((1, width))] * 2,
+        out_specs=[spec((tm, 4 * units), lambda i: (i, 0)), rows, rows, both_rows, both_cols, spec((16, tm), lambda i: (0, i))]
         + [fixed((slot, units))] * 4,
-        out_shape=[shape((tokens, width), BF), shape((tokens, width), F32), shape((2, tokens, LANES), BF),
-                   shape((2, LANES, tokens), BF), shape((16, tokens), BF)]
+        out_shape=[shape((tokens, 4 * units), BF), shape((tokens, width), BF), shape((tokens, width), BF),
+                   shape((2, tokens, LANES), BF), shape((2, LANES, tokens), BF), shape((16, tokens), BF)]
         + [shape((slot, units), BF)] * 4,
         scratch_shapes=[
             pltpu.VMEM((width, 4 * units), F32), pltpu.VMEM((width, 4 * units), F32),
@@ -528,26 +546,31 @@
         ],
         compiler_params=PARAMS,
         cost_estimate=cost(50),
-    )(owners, att, routes_t, gates, x, up, normed, *feeds, reduce_bias[None].astype(F32),
-      gain2, bias2)
-
-    def back_call(places, before, us):
+    )(owners, att, routes_t, gates, x, up, normed, *feeds, gain2, bias2)
+
+    half = tokens // 2
+
+    def back_call(places, before, us, carried=None):
+        carry = carried is not None
+        ends = [size for _, _, size in places]
+        ends[0] += carried.shape[0] if carry else 0
         many = sum(size for _, _, size in places)
         first = before is None
-        tq = 512
+        tq = half if many <= half else 512
         per = tokens // tq
         row_block = spec((1, tq, LANES), lambda i: (i // per, i % per, 0))
         col_block = spec((1, LANES, tq), lambda i: (i // per, 0, i % per))
         grad_block = spec((1, head, tq), lambda i: (i // per, 0, i % per))
         return pl.pallas_call(
-            functools.partial(attend_back_kernel, head=head, places=places, first=first),
+            functools.partial(attend_back_kernel, head=head, places=places, first=first, carry=carry),
             grid=(2 * per,),
             in_specs=[col_block, row_block, row_block] + [grad_block] * (not first)
+            + [fixed(carried.shape) for _ in range(carry)]
             + [spec((size, tq), lambda i, at=o * tokens // size + at: (at, i)) for o, at, size in places]
             + [spec((size, 2 * head), lambda i, at=at: (at, 0)) for _, at, size in places],
-            out_specs=[grad_block] + [fixed((size, 2 * head)) for _, _, size in places],
+            out_specs=[grad_block] + [fixed((size, 2 * head)) for size in ends],
             out_shape=[shape((2, head, tokens), F32)]
-            + [shape((size, 2 * head), BF) for _, _, size in places],
+            + [shape((size, 2 * head), BF) for size in ends],
             input_output_aliases={} if first else {3: 0},
             scratch_shapes=[
                 pltpu.VMEM((many, LANES), BF), pltpu.VMEM((head, many), BF),
@@ -555,24 +578,25 @@
             ],
             compiler_params=PARAMS,
             cost_estimate=cost(us),
-        )(do_t, do_rows, q_rows, *([] if first else [before]), *[kept] * len(places),
+        )(do_t, do_rows, q_rows, *([] if first else [before]), *([carried] if carry else []), *[kept] * len(places),
           *[pair[o] for o, _, _ in places])
 
     def by_holder(rows_of):
         each = rows_of.reshape(experts, head // 4, dp // experts, -1).transpose(0, 2, 1, 3)
         return each.reshape(dp, -1, width)
 
-    half = tokens // 2
-    arrived = [swapped(ffn[bit], bit) for bit in (3, 2, 1)]
-    q_grad, key3, key2, key0a = back_call(
-        [(3, 0, tokens), (2, 0, tokens), (0, 0, half)], None, 55
-    )
-    own = sum([a.astype(F32) for a in arrived], ffn[0].astype(F32)).astype(BF)
+    from3, from1 = swapped(ffn[3], 1), swapped(ffn[1], 1)
+    q_grad, key3a = back_call([(3, 0, half)], None, 11)
+    far, near = summed(ffn[2], from3), summed(ffn[0], from1)
+    q_grad, far, near = lax.optimization_barrier((q_grad, far, near))
+    from2 = swapped(far, 2)
+    q_grad, key3, key2 = back_call([(3, 1, half), (2, 0, tokens)], q_grad, 30, key3a)
+    own = summed(near, from2)
     own = jnp.concatenate([own[:tail].reshape(dp, -1, width), by_holder(own[tail:])], axis=1)
     q_grad, own, key3, key2 = lax.optimization_barrier((q_grad, own, key3, key2))
+    arrived = lax.all_to_all(own, "dp", split_axis=0, concat_axis=0, tiled=True)
     key_from3, key_from2 = swapped(key3, 3), swapped(key2, 2)
-    arrived = lax.all_to_all(own, "dp", split_axis=0, concat_axis=0, tiled=True)
-    q_grad, key1, key0b = back_call([(1, 0, tokens), (0, 1, half)], q_grad, 35)
+    q_grad, key1, key0 = back_call([(1, 0, tokens), (0, 0, tokens)], q_grad, 39)
     piece = jnp.sum(arrived.astype(F32), axis=0)
     q_grad, piece, key1 = lax.optimization_barrier((q_grad, piece, key1))
     key_from1 = swapped(key1, 1)
@@ -583,31 +607,42 @@
     rows = spec((tl, width), lambda i: (i, 0))
     cols2 = spec((2, tl), lambda i: (0, i))
     pair_rows = spec((tl, 2 * head), lambda i: (i, 0))
-    count = half // tl
-    first_rows = spec((tl, 2 * head), lambda i: (jnp.minimum(i, count - 1), 0))
-    second_rows = spec((tl, 2 * head), lambda i: (jnp.maximum(i - count, 0), 0))
-    input_grad, *last = pl.pallas_call(
+    normed_grad, *last = pl.pallas_call(
         functools.partial(last_kernel, head=head, experts=experts, scale=0.125),
         grid=(tokens // tl,),
-        in_specs=[SMEM, spec((2, head, tl), lambda i: (0, 0, i)), first_rows, second_rows, pair_rows, pair_rows,
-                  pair_rows,
-                  spec((16, tl), lambda i: (0, i)), cols2, rows, rows, rows, fixed((1, width)),
+        in_specs=[SMEM, spec((2, head, tl), lambda i: (0, 0, i)), pair_rows, pair_rows, pair_rows, pair_rows,
+                  spec((16, tl), lambda i: (0, i)), cols2, rows, rows,
                   fixed((experts * head, width)), fixed((width, 2 * head)), fixed((2 * experts, width))],
         out_specs=[rows] + [fixed((share + 48, width))] * 4,
-        out_shape=[shape((tokens, width), F32)] + [shape((share + 48, width), BF)] * 4,
+        out_shape=[shape((tokens, width), BF)] + [shape((share + 48, width), BF)] * 4,
         scratch_shapes=[
             pltpu.VMEM((experts * head, width), F32), pltpu.VMEM((2 * head, width), F32),
             pltpu.VMEM((8, width), F32),
         ],
         compiler_params=PARAMS,
         cost_estimate=cost(10),
-    )(owners, q_grad, key0a, key0b, key_from1, key_from2, key_from3, logit, routes_t, normed, x, mid_grad, gain1, wq,
+    )(owners, q_grad, key0, key_from1, key_from2, key_from3, logit, routes_t, normed, x, wq,
       shared_proj, router_t)
 
-    near, far = group_sum(last)
-    mine, total = lax.optimization_barrier((summed(near, far), total))
+    near, far = summed(last[0], swapped(last[1], 1)), summed(last[2], swapped(last[3], 1))
+    from2 = swapped(far, 2)
+    normed_grad, active, near = lax.optimization_barrier((normed_grad, active, near))
+    to = 512
+    rows = spec((to, width), lambda i: (i, 0))
+    block_out, input_grad = pl.pallas_call(
+        outputs_kernel,
+        grid=(tokens // to,),
+        in_specs=[spec((to, 4 * units), lambda i: (i, 0)), rows]
+        + [spec((units, width), lambda i: (width // units, 0))] * 4
+        + [fixed((1, width)), rows, rows, rows, fixed((1, width))],
+        out_specs=[rows, rows],
+        out_shape=[shape((tokens, width), BF), shape((tokens, width), F32)],
+        compiler_params=PARAMS,
+        cost_estimate=cost(10),
+    )(active, middle, *feeds, reduce_bias[None].astype(F32), normed_grad, x, mid_grad, gain1)
+    mine, total, input_grad = lax.optimization_barrier((summed(near, from2), total, input_grad))
     total = total.astype(F32)
-    ends = jnp.broadcast_to(mine[share:][None], (dp, 48, width))
+    ends = jnp.broadcast_to(mine[share : share + 40][None], (dp, 40, width))
     each = jnp.concatenate([by_holder(mine[:share]), ends], axis=1)
     got = lax.all_to_all(each, "dp", split_axis=0, concat_axis=0, tiled=True)
     got = jnp.sum(got.astype(F32), axis=0)
@@ -623,7 +658,7 @@
         block_out.reshape(1, tokens, width),
         input_grad.reshape(1, tokens, width),
         ends[each, :block],
-        ends[each + 1, :block],
+        ends[each, block : 2 * block],
         cut[8 : 8 + experts].T,
         shared_total.T,
         wq_total,

time: 279 us -> 266 us (0.953)
  waiting for transfers between devices: 41.2 us -> 22.5 us
  Pallas kernels: 179 us -> 186 us
    ppermute x18 -> x15, waiting for transfers between devices: 26.2 us -> 3.13 us  [swapped(): return lax.ppermute(value, 'mp', [(i, i ^ bit) for i in range(4)])]
    pallas_call x0 -> x1, Pallas kernels: none -> 11.8 us  [on_device(): pl.pallas_call(outputs_kernel, grid=(tokens // to,), in_specs=[spec((to,...]
    all_to_all x2 -> x3, waiting for transfers between devices: 5.43 us -> 11.4 us  [sent_to_all(): return lax.all_to_all(wide, axes, split_axis=0, concat_axis=0, tiled=True)]
    pallas_call x1, Pallas kernels: 46.4 us -> 41.3 us  [on_device(): pl.pallas_call(functools.partial(middle_kernel, head=head, experts=expert...]
    all_to_all x2 -> x3, starting transfers between devices: 13.2 us -> 16.6 us  [sent_to_all(): return lax.all_to_all(wide, axes, split_axis=0, concat_axis=0, tiled=True)]
    ppermute x18 -> x15, starting transfers between devices: 12.5 us -> 9.17 us  [swapped(): return lax.ppermute(value, 'mp', [(i, i ^ bit) for i in range(4)])]
    pallas_call x2 -> x3, Pallas kernels: 76.9 us -> 79.6 us  [back_call(): pl.pallas_call(functools.partial(attend_back_kernel, head=head, places=pl...]
    unnamed x42 -> x38, local copies, waits for them, and re-layouts: 5.62 us -> 5.6 us
  transfers between devices with their start and end apart: 22 -> 20, of which waited for: 9 -> 6; matrix products, arithmetic and copies ran while one was open for 4% -> 4% of each run, Pallas kernels for 48% -> 54%
where the time goes in v1:
time: 266 us
  Pallas kernels  186 us (70%)
  starting transfers between devices  34.3 us (13%)
  waiting for transfers between devices  22.5 us (8%)
  local copies, waits for them, and re-layouts  14.4 us (5%)
  other arithmetic  6.64 us (2%)
    pallas_call x3, Pallas kernels, back_call(): pl.pallas_call(functools.partial(attend_back_kernel, head=head, places=pl...  79.6 us
    pallas_call x1, Pallas kernels, on_device(): pl.pallas_call(functools.partial(middle_kernel, head=head, experts=expert...  41.3 us
    pallas_call x1, Pallas kernels, on_device(): pl.pallas_call(functools.partial(attend_kernel, head=head, span=4 * token...  34.7 us
    all_to_all x3, starting transfers between devices, sent_to_all(): return lax.all_to_all(wide, axes, split_axis=0, concat_axis=0, tiled=True)  16.6 us
    pallas_call x1, Pallas kernels, on_device(): pl.pallas_call(outputs_kernel, grid=(tokens // to,), in_specs=[spec((to,...  11.8 us
    all_to_all x3, waiting for transfers between devices, sent_to_all(): return lax.all_to_all(wide, axes, split_axis=0, concat_axis=0, tiled=True)  11.4 us
    ppermute x15, starting transfers between devices, swapped(): return lax.ppermute(value, 'mp', [(i, i ^ bit) for i in range(4)])  9.17 us
    pallas_call x1, Pallas kernels, on_device(): pl.pallas_call(functools.partial(last_kernel, head=head, experts=experts,...  8.42 us
  transfers between devices with their start and end apart: 20, of which 6 were waited for; matrix products, arithmetic and copies ran while one was open for 4% of the time, Pallas kernels for 54%

profile of v1, /device:TPU:0, one launch (start us, length us, event | category | flops | bytes accessed | tf_op | source)
XLA Modules:
  0.0 265.6 jit_solution(18196246035176480606)
XLA Ops:
  0.7 1.6 broadcast_in_dim.19
  2.2 7.3 %all-to-all-start = ((bf16[32,16,512]{2,1,0:T(8,128)(2,1)}), bf16[32,16,512]{2,1,0:T(8,128)(2,1)S(1)}, u32[]{:S(2)}, u32[]{:S(2)}) async-start(bf16[32,16,512]{2,1,0:T(8,128)(2,1)} %broadcast_in_dim.19), calls=%async_computation | async-start | bytes 1048576 | tf_op jit(solution)/shard_map/all_to_all | solution.py:410
  10.2 5.2 %shard_map.263 = (bf16[2048,512]{1,0:T(8,128)(2,1)}, bf16[2048,128]{1,0:T(8,128)(2,1)}, f32[2,2048]{1,0:T(2,128)}) custom-call(bf16[2048,512]{1,0:T(8,128)(2,1)} %bitcast.50, f32[1,512]{1,0:T(1,128)} %bitcast.61, f32[1,512]{1,0:T(1,128)} %bitcast.58, bf16[16,512]{1,0:T(8,128)(2,1)} %pad.4.router, bf16[512,128]{1,0:T(8,128)(2,1)} %proj.3, s32[2,2048]{1,0:T(2,128)} %bitcast.54), custom_call_target="tpu_custom_call" | custom-call | flops 5500000256 | bytes 1024 | tf_op jit(solution)/shard_map/pallas_call | solution.py:469
  15.4 1.8 collective-permute-start
  17.1 7.9 %all-to-all-done = bf16[32,16,512]{2,1,0:T(8,128)(2,1)S(1)} async-done(((bf16[32,16,512]{2,1,0:T(8,128)(2,1)}), bf16[32,16,512]{2,1,0:T(8,128)(2,1)S(1)}, u32[]{:S(2)}, u32[]{:S(2)}) %all-to-all-start) | async-done | bytes 524320 | tf_op jit(solution)/shard_map/all_to_all | solution.py:410
  25.8 3.4 %all-to-all-start.1 = ((bf16[8,16,512]{2,1,0:T(8,128)(2,1)}), bf16[8,16,512]{2,1,0:T(8,128)(2,1)S(1)}, u32[]{:S(2)}, u32[]{:S(2)}) async-start(bf16[8,16,512]{2,1,0:T(8,128)(2,1)} %broadcast_in_dim.20), calls=%async_computation.1 | async-start | bytes 262144 | tf_op jit(solution)/shard_map/all_to_all | solution.py:410
  29.2 5.1 %shard_map.264 = (bf16[2,64,2048]{2,1,0:T(8,128)(2,1)}, bf16[2,2048,128]{2,1,0:T(8,128)(2,1)}) custom-call(bf16[2048,512]{1,0:T(8,128)(2,1)} %get-tuple-element.70.normed, bf16[512,512]{1,0:T(8,128)(2,1)} %bitcast.44, s32[2,2048]{1,0:T(2,128)} %bitcast.55), custom_call_target="tpu_custom_call" | custom-call | flops 5500000256 | bytes 1024 | tf_op jit(solution)/shard_map/pallas_call | solution.py:486
  34.3 2.2 all-to-all-done.1
  37.9 1.4 collective-permute-start.4
  40.3 34.7 %shard_map.265 = (f32[2,72,2048]{2,1,0:T(8,128)}, bf16[8192,4096]{1,0:T(8,128)(2,1)}) custom-call(s32[4]{0:T(128)} %iota_xor_fusion.where, s32[1]{0:T(128)S(6)} %copy.42.length, bf16[2,64,2048]{2,1,0:T(8,128)(2,1)} %get-tuple-element.73.q, bf16[2048,128]{1,0:T(8,128)(2,1)} %get-tuple-element.69.p0.rest_4_, ...), custom_call_target="tpu_custom_call" | custom-call | flops 36300001280 | bytes 1024 | tf_op jit(solution)/shard_map/pallas_call | solution.py:504
  75.3 2.6 collective-permute-done.5.f3.r3
  78.9 41.3 %shard_map.266 = (bf16[2048,2048]{1,0:T(8,128)(2,1)}, bf16[2048,512]{1,0:T(8,128)(2,1)}, bf16[2048,512]{1,0:T(8,128)(2,1)}, bf16[2,2048,128]{2,1,0:T(8,128)(2,1)...) custom-call(s32[4]{0:T(128)} %iota_xor_fusion.where, ...), custom_call_target="tpu_custom_call" | custom-call | flops 54999998464 | bytes 1024 | tf_op jit(solution)/shard_map/pallas_call | solution.py:531
  120.8 11.8 %shard_map.267 = (f32[2,64,2048]{2,1,0:T(8,128)}, bf16[1024,128]{1,0:T(8,128)(2,1)}) custom-call(bf16[2,128,2048]{2,1,0:T(8,128)(2,1)} %get-tuple-element.79.dot, bf16[2,2048,128]{2,1,0:T(8,128)(2,1)} %get-tuple-element.80.do, bf16[2,2048,128]{2,1,0:T(8,128)(2,1)} %get-tuple-element.81.q, ...), custom_call_target="tpu_custom_call" | custom-call | flops 12099999744 | bytes 1024 | tf_op jit(solution)/shard_map/pallas_call | solution.py:564
  134.9 29.7 %shard_map.268 = (f32[2,64,2048]{2,1,0:T(8,128)}, bf16[2048,128]{1,0:T(8,128)(2,1)}, bf16[2048,128]{1,0:T(8,128)(2,1)}) custom-call(bf16[2,128,2048]{2,1,0:T(8,128)(2,1)} %get-tuple-element.79.dot, bf16[2,2048,128]{2,1,0:T(8,128)(2,1)} %get-tuple-element.80.do, bf16[2,2048,128]{2,1,0:T(8,128)(2,1)} %get-tuple-element.81.q, ...), custom_call_target="tpu_custom_call", output_to_operand_aliasing={{0}: (3, {})} | custom-call | flops 32999999488 | bytes 1024 | tf_op jit(solution)/shard_map/pallas_call | solution.py:564
  166.2 3.9 %all-to-all-start.2 = ((bf16[8,152,512]{2,1,0:T(8,128)(2,1)}), bf16[8,152,512]{2,1,0:T(8,128)(2,1)S(1)}, u32[]{:S(2)}, u32[]{:S(2)}) async-start(bf16[8,152,512]{2,1,0:T(8,128)(2,1)} %pad_maximum_fusion), calls=%async_computation.2 | async-start | bytes 2490368 | tf_op jit(solution)/shard_map/all_to_all | solution.py:597
  170.0 1.3 collective-permute-start.10
  171.4 38.1 %shard_map.269 = (f32[2,64,2048]{2,1,0:T(8,128)}, bf16[2048,128]{1,0:T(8,128)(2,1)}, bf16[2048,128]{1,0:T(8,128)(2,1)}) custom-call(bf16[2,128,2048]{2,1,0:T(8,128)(2,1)} %get-tuple-element.79.dot, bf16[2,2048,128]{2,1,0:T(8,128)(2,1)} %get-tuple-element.80.do, bf16[2,2048,128]{2,1,0:T(8,128)(2,1)} %get-tuple-element.81.q, ...), custom_call_target="tpu_custom_call", output_to_operand_aliasing={{0}: (3, {})} | custom-call | flops 42900000768 | bytes 1024 | tf_op jit(solution)/shard_map/pallas_call | solution.py:564
  211.7 5.9 %all-to-all-start.3 = ((bf16[8,136,512]{2,1,0:T(8,128)(2,1)}), bf16[8,136,512]{2,1,0:T(8,128)(2,1)S(1)}, u32[]{:S(2)}, u32[]{:S(2)}) async-start(bf16[8,136,512]{2,1,0:T(8,128)(2,1)} %broadcast_in_dim.50), calls=%async_computation.3 | async-start | bytes 2228224 | tf_op jit(solution)/shard_map/all_to_all | solution.py:410
  218.4 8.4 %shard_map.270 = (bf16[2048,512]{1,0:T(8,128)(2,1)}, bf16[176,512]{1,0:T(8,128)(2,1)}, bf16[176,512]{1,0:T(8,128)(2,1)}, bf16[176,512]{1,0:T(8,128)(2,1)}, bf16[176,512]{1,0:T(8,128)(2,1)}) custom-call(s32[4]{0:T(128)} %iota_xor_fusion.where, f32[2,64,2048]{2,1,0:T(8,128)} %get-tuple-element.99.dq, bf16[2048,128]{1,0:T(8,128)(2,1)} %get-tuple-element.100.p0, ...), custom_call_target="tpu_custom_call" | custom-call | flops 11000000512 | bytes 1024 | tf_op jit(solution)/shard_map/pallas_call | solution.py:610
  231.8 11.8 %shard_map.271 = (bf16[2048,512]{1,0:T(8,128)(2,1)}, f32[2048,512]{1,0:T(8,128)}) custom-call(bf16[2048,2048]{1,0:T(8,128)(2,1)} %get-tuple-element.109.active, bf16[2048,512]{1,0:T(8,128)(2,1)} %get-tuple-element.110.middle, bf16[1168,512]{1,0:T(8,128)(2,1)} %copy-done.3, bf16[1168,512]{1,0:T(8,128)(2,1)} %copy-done.13, bf16[1168,512]{1,0:T(8,128)(2,1)} %copy-done.12, ...), custom_call_target="tpu_custom_call" | custom-call | flops 11000000512 | bytes 1024 | tf_op jit(solution)/shard_map/pallas_call | solution.py:632
  243.6 1.3 all-to-all-done.3
  245.8 4.7 %all-to-all-start.4 = ((bf16[8,56,512]{2,1,0:T(8,128)(2,1)}), bf16[8,56,512]{2,1,0:T(8,128)(2,1)S(1)}, u32[]{:S(2)}, u32[]{:S(2)}) async-start(bf16[8,56,512]{2,1,0:T(8,128)(2,1)} %pad_maximum_fusion.2), calls=%async_computation.4 | async-start | bytes 917504 | tf_op jit(solution)/shard_map/all_to_all | solution.py:647
  253.2 1.3 copy.39
  255.7 7.9 %all-to-all-done.4 = bf16[8,56,512]{2,1,0:T(8,128)(2,1)S(1)} async-done(((bf16[8,56,512]{2,1,0:T(8,128)(2,1)}), bf16[8,56,512]{2,1,0:T(8,128)(2,1)S(1)}, u32[]{:S(2)}, u32[]{:S(2)}) %all-to-all-start.4) | async-done | bytes 458784 | tf_op jit(solution)/shard_map/all_to_all | solution.py:647
  (99 shorter events, 23.4 us)
Async XLA Ops:
  0.6 8.9 %copy-start.9 = (bf16[512,8]{0,1:T(8,128)(2,1)S(1)}, bf16[512,8]{0,1:T(8,128)(2,1)}, u32[]{:S(2)}) copy-start(bf16[512,8]{0,1:T(8,128)(2,1)} %param.21) | copy-start | bytes 24580
  2.2 22.9 %all-to-all-start = ((bf16[32,16,512]{2,1,0:T(8,128)(2,1)}), bf16[32,16,512]{2,1,0:T(8,128)(2,1)S(1)}, u32[]{:S(2)}, u32[]{:S(2)}) async-start(bf16[32,16,512]{2,1,0:T(8,128)(2,1)} %broadcast_in_dim.19), calls=%async_computation | async-start | bytes 1048576 | tf_op jit(solution)/shard_map/all_to_all | solution.py:410
  10.2 14.9 %copy-start.8 = (bf16[16,512]{1,0:T(8,128)(2,1)S(1)}, bf16[16,512]{1,0:T(8,128)(2,1)}, u32[]{:S(2)}) copy-start(bf16[16,512]{1,0:T(8,128)(2,1)} %param.24) | copy-start | bytes 49156
  15.4 21.2 %collective-permute-start = (bf16[2048,128]{1,0:T(8,128)(2,1)}, bf16[2048,128]{1,0:T(8,128)(2,1)S(1)}, u32[]{:S(2)}, u32[]{:S(2)}) collective-permute-start(bf16[2048,128]{1,0:T(8,128)(2,1)} %get-tuple-element.69.p0.rest_4_), channel_id=1, source_target_pairs={{0,2},{1,3},{2,0},{3,1},{4,6},{5,7},{6,4},{7,5},{8,10},{9,11},{10,... | collective-permute-start | bytes 1572872 | tf_op jit(solution)/shard_map/ppermute | solution.py:395
  17.1 22.3 %collective-permute-start.1 = (bf16[2048,128]{1,0:T(8,128)(2,1)}, bf16[2048,128]{1,0:T(8,128)(2,1)}, u32[]{:S(2)}, u32[]{:S(2)}) collective-permute-start(bf16[2048,128]{1,0:T(8,128)(2,1)} %get-tuple-element.69.p0.rest_4_), channel_id=1, source_target_pairs={{0,1},{1,0},{2,3},{3,2},{4,5},{5,4},{6,7},{7,6},{8,9},{9,8},{10,11... | collective-permute-start | bytes 1572872 | tf_op jit(solution)/shard_map/ppermute | solution.py:395
  25.8 10.7 %all-to-all-start.1 = ((bf16[8,16,512]{2,1,0:T(8,128)(2,1)}), bf16[8,16,512]{2,1,0:T(8,128)(2,1)S(1)}, u32[]{:S(2)}, u32[]{:S(2)}) async-start(bf16[8,16,512]{2,1,0:T(8,128)(2,1)} %broadcast_in_dim.20), calls=%async_computation.1 | async-start | bytes 262144 | tf_op jit(solution)/shard_map/all_to_all | solution.py:410
  36.6 38.3 %copy-start.3 = (bf16[1168,512]{1,0:T(8,128)(2,1)}, bf16[1168,512]{1,0:T(8,128)(2,1)S(1)}, u32[]{:S(2)}) copy-start(bf16[1168,512]{1,0:T(8,128)(2,1)S(1)} %pad_maximum_fusion.1.f0.r0) | copy-start | bytes 3588100
  36.6 2.9 %collective-permute-start.2 = (bf16[2048,128]{1,0:T(8,128)(2,1)S(1)}, bf16[2048,128]{1,0:T(8,128)(2,1)S(1)}, u32[]{:S(2)}, u32[]{:S(2)}) collective-permute-start(bf16[2048,128]{1,0:T(8,128)(2,1)S(1)} %collective-permute-done.p2.rest_5_), channel_id=1, source_target_pairs={{0,1},{1,0},{2,3},{3,2},{4,5},{5,4},{6,7},{7,6},{8,9},{9,8},{10,11... | collective-permute-start | bytes 1572872 | tf_op jit(solution)/shard_map/ppermute | solution.py:395
  37.9 37.1 %collective-permute-start.4 = (bf16[1168,512]{1,0:T(8,128)(2,1)S(1)}, bf16[1168,512]{1,0:T(8,128)(2,1)S(1)}, u32[]{:S(2)}, u32[]{:S(2)}) collective-permute-start(bf16[1168,512]{1,0:T(8,128)(2,1)S(1)} %pad_maximum_fusion.1.f0.r0), channel_id=1, source_target_pairs={{0,2},{1,3},{2,0},{3,1},{4,6},{5,7},{6,4},{7,5},{8,10},{9,11},{10,... | collective-permute-start | bytes 3588104 | tf_op jit(solution)/shard_map/ppermute | solution.py:395
  39.3 36.0 %collective-permute-start.3 = (bf16[1168,512]{1,0:T(8,128)(2,1)S(1)}, bf16[1168,512]{1,0:T(8,128)(2,1)S(1)}, u32[]{:S(2)}, u32[]{:S(2)}) collective-permute-start(bf16[1168,512]{1,0:T(8,128)(2,1)S(1)} %pad_maximum_fusion.1.f0.r0), channel_id=1, source_target_pairs={{0,1},{1,0},{2,3},{3,2},{4,5},{5,4},{6,7},{7,6},{8,9},{9,8},{10,11... | collective-permute-start | bytes 3588104 | tf_op jit(solution)/shard_map/ppermute | solution.py:395
  74.9 2.9 %collective-permute-start.5 = (bf16[1168,512]{1,0:T(8,128)(2,1)S(1)}, bf16[1168,512]{1,0:T(8,128)(2,1)S(1)}, u32[]{:S(2)}, u32[]{:S(2)}) collective-permute-start(bf16[1168,512]{1,0:T(8,128)(2,1)S(1)} %collective-permute-done.4.f2.r2), channel_id=1, source_target_pairs={{0,1},{1,0},{2,3},{3,2},{4,5},{5,4},{6,7},{7,6},{8,9},{9,8},{10,11... | collective-permute-start | bytes 3588104 | tf_op jit(solution)/shard_map/ppermute | solution.py:395
  120.2 12.3 %collective-permute-start.7 = (bf16[1216,512]{1,0:T(8,128)(2,1)}, bf16[1216,512]{1,0:T(8,128)(2,1)S(1)}, u32[]{:S(2)}, u32[]{:S(2)}) collective-permute-start(bf16[1216,512]{1,0:T(8,128)(2,1)} %get-tuple-element.87), channel_id=1, source_target_pairs={{0,1},{1,0},{2,3},{3,2},{4,5},{5,4},{6,7},{7,6},{8,9},{9,8},{10,11... | collective-permute-start | bytes 3735560 | tf_op jit(solution)/shard_map/ppermute | solution.py:395
  120.6 12.3 %collective-permute-start.6 = (bf16[1216,512]{1,0:T(8,128)(2,1)}, bf16[1216,512]{1,0:T(8,128)(2,1)S(1)}, u32[]{:S(2)}, u32[]{:S(2)}) collective-permute-start(bf16[1216,512]{1,0:T(8,128)(2,1)} %get-tuple-element.85), channel_id=1, source_target_pairs={{0,1},{1,0},{2,3},{3,2},{4,5},{5,4},{6,7},{7,6},{8,9},{9,8},{10,11... | collective-permute-start | bytes 3735560 | tf_op jit(solution)/shard_map/ppermute | solution.py:395
  120.8 11.8 %copy-start.2 = (bf16[1216,512]{1,0:T(8,128)(2,1)S(1)}, bf16[1216,512]{1,0:T(8,128)(2,1)}, u32[]{:S(2)}) copy-start(bf16[1216,512]{1,0:T(8,128)(2,1)} %get-tuple-element.86) | copy-start | bytes 3735556
  134.2 30.4 %collective-permute-start.8 = (bf16[1216,512]{1,0:T(8,128)(2,1)S(1)}, bf16[1216,512]{1,0:T(8,128)(2,1)S(1)}, u32[]{:S(2)}, u32[]{:S(2)}) collective-permute-start(bf16[1216,512]{1,0:T(8,128)(2,1)S(1)} %add_convert_fusion.2), channel_id=1, source_target_pairs={{0,2},{1,3},{2,0},{3,1},{4,6},{5,7},{6,4},{7,5},{8,10},{9,11},{10,... | collective-permute-start | bytes 3735560 | tf_op jit(solution)/shard_map/ppermute | solution.py:395
  166.2 43.4 %all-to-all-start.2 = ((bf16[8,152,512]{2,1,0:T(8,128)(2,1)}), bf16[8,152,512]{2,1,0:T(8,128)(2,1)S(1)}, u32[]{:S(2)}, u32[]{:S(2)}) async-start(bf16[8,152,512]{2,1,0:T(8,128)(2,1)} %pad_maximum_fusion), calls=%async_computation.2 | async-start | bytes 2490368 | tf_op jit(solution)/shard_map/all_to_all | solution.py:597
  170.0 47.6 %collective-permute-start.10 = (bf16[2048,128]{1,0:T(8,128)(2,1)S(1)}, bf16[2048,128]{1,0:T(8,128)(2,1)S(1)}, u32[]{:S(2)}, u32[]{:S(2)}) collective-permute-start(bf16[2048,128]{1,0:T(8,128)(2,1)S(1)} %copy-done.16), channel_id=1, source_target_pairs={{0,2},{1,3},{2,0},{3,1},{4,6},{5,7},{6,4},{7,5},{8,10},{9,11},{10,... | collective-permute-start | bytes 1572872 | tf_op jit(solution)/shard_map/ppermute | solution.py:395
  171.3 46.3 %collective-permute-start.11 = (bf16[2048,128]{1,0:T(8,128)(2,1)S(1)}, bf16[2048,128]{1,0:T(8,128)(2,1)}, u32[]{:S(2)}, u32[]{:S(2)}) collective-permute-start(bf16[2048,128]{1,0:T(8,128)(2,1)S(1)} %copy-done.15), channel_id=1, source_target_pairs={{0,3},{1,2},{2,1},{3,0},{4,7},{5,6},{6,5},{7,4},{8,11},{9,10},{10,... | collective-permute-start | bytes 1572872 | tf_op jit(solution)/shard_map/ppermute | solution.py:395
  209.7 7.9 %collective-permute-start.9 = (bf16[2048,128]{1,0:T(8,128)(2,1)}, bf16[2048,128]{1,0:T(8,128)(2,1)}, u32[]{:S(2)}, u32[]{:S(2)}) collective-permute-start(bf16[2048,128]{1,0:T(8,128)(2,1)} %get-tuple-element.101), channel_id=1, source_target_pairs={{0,1},{1,0},{2,3},{3,2},{4,5},{5,4},{6,7},{7,6},{8,9},{9,8},{10,11... | collective-permute-start | bytes 1572872 | tf_op jit(solution)/shard_map/ppermute | solution.py:395
  211.7 33.3 %all-to-all-start.3 = ((bf16[8,136,512]{2,1,0:T(8,128)(2,1)}), bf16[8,136,512]{2,1,0:T(8,128)(2,1)S(1)}, u32[]{:S(2)}, u32[]{:S(2)}) async-start(bf16[8,136,512]{2,1,0:T(8,128)(2,1)} %broadcast_in_dim.50), calls=%async_computation.3 | async-start | bytes 2228224 | tf_op jit(solution)/shard_map/all_to_all | solution.py:410
  226.9 1.7 collective-permute-start.13
  227.5 3.3 %collective-permute-start.12 = (bf16[176,512]{1,0:T(8,128)(2,1)}, bf16[176,512]{1,0:T(8,128)(2,1)S(1)}, u32[]{:S(2)}, u32[]{:S(2)}) collective-permute-start(bf16[176,512]{1,0:T(8,128)(2,1)} %get-tuple-element.108), channel_id=1, source_target_pairs={{0,1},{1,0},{2,3},{3,2},{4,5},{5,4},{6,7},{7,6},{8,9},{9,8},{10,11... | collective-permute-start | bytes 540680 | tf_op jit(solution)/shard_map/ppermute | solution.py:395
  229.5 14.1 %collective-permute-start.14 = (bf16[176,512]{1,0:T(8,128)(2,1)S(1)}, bf16[176,512]{1,0:T(8,128)(2,1)S(1)}, u32[]{:S(2)}, u32[]{:S(2)}) collective-permute-start(bf16[176,512]{1,0:T(8,128)(2,1)S(1)} %add_convert_fusion.4), channel_id=1, source_target_pairs={{0,2},{1,3},{2,0},{3,1},{4,6},{5,7},{6,4},{7,5},{8,10},{9,11},{10,... | collective-permute-start | bytes 540680 | tf_op jit(solution)/shard_map/ppermute | solution.py:395
  245.8 17.8 %all-to-all-start.4 = ((bf16[8,56,512]{2,1,0:T(8,128)(2,1)}), bf16[8,56,512]{2,1,0:T(8,128)(2,1)S(1)}, u32[]{:S(2)}, u32[]{:S(2)}) async-start(bf16[8,56,512]{2,1,0:T(8,128)(2,1)} %pad_maximum_fusion.2), calls=%async_computation.4 | async-start | bytes 917504 | tf_op jit(solution)/shard_map/all_to_all | solution.py:647
  (14 other events, 55.8 us)

commit v2 on v1

--- a/solution.py
+++ b/solution.py
@@ -10,8 +10,8 @@
 F32 = jnp.float32
 BF = jnp.bfloat16
 EPS = 1e-05
-LOG2E = 1.4426950408889634
-LN2 = 0.6931471805599453
+SCALE = 0.125
+TO_EXP2 = SCALE * 1.4426950408889634
 MASKED = -1e30
 GELU_A = 0.7978845608028654
 GELU_B = 0.044715
@@ -111,8 +111,8 @@
     gates[1:2, :] = up1 * inverse
 
 
-def query_kernel(normed, table, routes, queries, q_rows, *, experts, scale):
-    every = nt(table[...], normed[...]) * scale
+def query_kernel(normed, table, routes, queries, q_rows, *, experts):
+    every = nt(table[...], normed[...])
     for s in range(2):
         one = picked(every, routes[s : s + 1, :], experts)
         queries[s] = one.astype(BF)
@@ -154,7 +154,7 @@
     query = q[0]
     wide = query.astype(F32)
     length = jnp.sqrt(jnp.sum(wide * wide, axis=0, keepdims=True))
-    bound = length * limit[0:1, 0:1]
+    bound = length * limit[0:1, 0:1] * TO_EXP2
     top[...] = jnp.zeros_like(top)
     n = query.shape[1]
     rest = jnp.zeros((LANES - head - 16, n), BF)
@@ -177,7 +177,7 @@
     total = jnp.zeros((LANES, n), F32)
     for j in range(4 * part // span):
         here = slice(j * span, (j + 1) * span)
-        weights = jnp.exp2(nn(keys[here, :], extended)).astype(BF)
+        weights = jnp.exp2(nn(keys[here, :], extended) * TO_EXP2).astype(BF)
         kept[here, :] = weights
         total = total + nn(values[:, here], weights)
     inverse = 1.0 / total[head : head + 1, :]
@@ -229,7 +229,7 @@
                 grad[0:at, :] = carried[...]
             size = sizes[n]
             lane = lax.broadcasted_iota(jnp.int32, (size, LANES), 1)
-            grad[at : at + size, :] = (both[here, :] * jnp.where(lane < head, LN2, 1.0)).astype(BF)
+            grad[at : at + size, :] = (both[here, :] * jnp.where(lane < head, SCALE, 1.0)).astype(BF)
 
 
 def middle_kernel(
@@ -333,7 +333,7 @@
 
 def last_kernel(
     where, dq, p0, p1, p2, p3, logit, routes, normed, x, wq, proj, router,
-    out, s0, s1, s2, s3, wq_sum, sp_sum, small, *, head, experts, scale,
+    out, s0, s1, s2, s3, wq_sum, sp_sum, small, *, head, experts,
 ):
     step = pl.program_id(0)
 
@@ -343,7 +343,7 @@
             r[...] = jnp.zeros_like(r)
 
     route0, route1 = routes[0:1, :], routes[1:2, :]
-    grad0, grad1 = dq[0] * scale, dq[1] * scale
+    grad0, grad1 = dq[0] * SCALE, dq[1] * SCALE
     placed = spread(grad0, grad1, route0, route1, experts).astype(BF)
     own = p0[...].astype(F32)
     for p in (p1, p2, p3):
@@ -484,7 +484,7 @@
     o_share = o_share.reshape(experts, dp // experts, head // 4, -1).transpose(0, 2, 1, 3)
     o_share = o_share.reshape(experts * head // 4, width)
     queries, q_rows = pl.pallas_call(
-        functools.partial(query_kernel, experts=experts, scale=0.125 * LOG2E),
+        functools.partial(query_kernel, experts=experts),
         grid=(tokens // tb,),
         in_specs=[rows, fixed((experts * head, width)), cols2],
         out_specs=[spec((2, head, tb), lambda i: (0, 0, i)), spec((2, tb, LANES), lambda i: (0, i, 0))],
@@ -608,7 +608,7 @@
     cols2 = spec((2, tl), lambda i: (0, i))
     pair_rows = spec((tl, 2 * head), lambda i: (i, 0))
     normed_grad, *last = pl.pallas_call(
-        functools.partial(last_kernel, head=head, experts=experts, scale=0.125),
+        functools.partial(last_kernel, head=head, experts=experts),
         grid=(tokens // tl,),
         in_specs=[SMEM, spec((2, head, tl), lambda i: (0, 0, i)), pair_rows, pair_rows, pair_rows, pair_rows,
                   spec((16, tl), lambda i: (0, i)), cols2, rows, rows,

time: 266 us -> 266 us (level)
  no operation moved by 1% of the time
where the time goes in v2:
time: 266 us
  Pallas kernels  186 us (70%)
  starting transfers between devices  34.3 us (13%)
  waiting for transfers between devices  22.5 us (8%)
  local copies, waits for them, and re-layouts  14.4 us (5%)
  other arithmetic  6.64 us (2%)
    pallas_call x3, Pallas kernels, back_call(): pl.pallas_call(functools.partial(attend_back_kernel, head=head, places=pl...  79.6 us
    pallas_call x1, Pallas kernels, on_device(): pl.pallas_call(functools.partial(middle_kernel, head=head, experts=expert...  41.3 us
    pallas_call x1, Pallas kernels, on_device(): pl.pallas_call(functools.partial(attend_kernel, head=head, span=4 * token...  34.7 us
    all_to_all x3, starting transfers between devices, sent_to_all(): return lax.all_to_all(wide, axes, split_axis=0, concat_axis=0, tiled=True)  16.6 us
    pallas_call x1, Pallas kernels, on_device(): pl.pallas_call(outputs_kernel, grid=(tokens // to,), in_specs=[spec((to,...  11.8 us
    all_to_all x3, waiting for transfers between devices, sent_to_all(): return lax.all_to_all(wide, axes, split_axis=0, concat_axis=0, tiled=True)  11.4 us
    ppermute x15, starting transfers between devices, swapped(): return lax.ppermute(value, 'mp', [(i, i ^ bit) for i in range(4)])  9.21 us
    pallas_call x1, Pallas kernels, on_device(): pl.pallas_call(functools.partial(last_kernel, head=head, experts=experts)...  8.42 us
  transfers between devices with their start and end apart: 20, of which 6 were waited for; matrix products, arithmetic and copies ran while one was open for 4% of the time, Pallas kernels for 54%

profile of v2, /device:TPU:0, one launch (start us, length us, event | category | flops | bytes accessed | tf_op | source)
XLA Modules:
  0.0 265.6 jit_solution(9712382334791432842)
XLA Ops:
  0.7 1.6 broadcast_in_dim.19
  2.2 7.3 %all-to-all-start = ((bf16[32,16,512]{2,1,0:T(8,128)(2,1)}), bf16[32,16,512]{2,1,0:T(8,128)(2,1)S(1)}, u32[]{:S(2)}, u32[]{:S(2)}) async-start(bf16[32,16,512]{2,1,0:T(8,128)(2,1)} %broadcast_in_dim.19), calls=%async_computation | async-start | bytes 1048576 | tf_op jit(solution)/shard_map/all_to_all | solution.py:410
  10.2 5.2 %shard_map.263 = (bf16[2048,512]{1,0:T(8,128)(2,1)}, bf16[2048,128]{1,0:T(8,128)(2,1)}, f32[2,2048]{1,0:T(2,128)}) custom-call(bf16[2048,512]{1,0:T(8,128)(2,1)} %bitcast.50, f32[1,512]{1,0:T(1,128)} %bitcast.61, f32[1,512]{1,0:T(1,128)} %bitcast.58, bf16[16,512]{1,0:T(8,128)(2,1)} %pad.4.router, bf16[512,128]{1,0:T(8,128)(2,1)} %proj.3, s32[2,2048]{1,0:T(2,128)} %bitcast.54), custom_call_target="tpu_custom_call" | custom-call | flops 5500000256 | bytes 1024 | tf_op jit(solution)/shard_map/pallas_call | solution.py:469
  15.4 1.8 collective-permute-start
  17.1 7.9 %all-to-all-done = bf16[32,16,512]{2,1,0:T(8,128)(2,1)S(1)} async-done(((bf16[32,16,512]{2,1,0:T(8,128)(2,1)}), bf16[32,16,512]{2,1,0:T(8,128)(2,1)S(1)}, u32[]{:S(2)}, u32[]{:S(2)}) %all-to-all-start) | async-done | bytes 524320 | tf_op jit(solution)/shard_map/all_to_all | solution.py:410
  25.8 3.4 %all-to-all-start.1 = ((bf16[8,16,512]{2,1,0:T(8,128)(2,1)}), bf16[8,16,512]{2,1,0:T(8,128)(2,1)S(1)}, u32[]{:S(2)}, u32[]{:S(2)}) async-start(bf16[8,16,512]{2,1,0:T(8,128)(2,1)} %broadcast_in_dim.20), calls=%async_computation.1 | async-start | bytes 262144 | tf_op jit(solution)/shard_map/all_to_all | solution.py:410
  29.2 5.1 %shard_map.264 = (bf16[2,64,2048]{2,1,0:T(8,128)(2,1)}, bf16[2,2048,128]{2,1,0:T(8,128)(2,1)}) custom-call(bf16[2048,512]{1,0:T(8,128)(2,1)} %get-tuple-element.70.normed, bf16[512,512]{1,0:T(8,128)(2,1)} %bitcast.44, s32[2,2048]{1,0:T(2,128)} %bitcast.55), custom_call_target="tpu_custom_call" | custom-call | flops 5500000256 | bytes 1024 | tf_op jit(solution)/shard_map/pallas_call | solution.py:486
  34.3 2.2 all-to-all-done.1
  37.9 1.4 collective-permute-start.4
  40.3 34.7 %shard_map.265 = (f32[2,72,2048]{2,1,0:T(8,128)}, bf16[8192,4096]{1,0:T(8,128)(2,1)}) custom-call(s32[4]{0:T(128)} %iota_xor_fusion.where, s32[1]{0:T(128)S(6)} %copy.42.length, bf16[2,64,2048]{2,1,0:T(8,128)(2,1)} %get-tuple-element.73.q, bf16[2048,128]{1,0:T(8,128)(2,1)} %get-tuple-element.69.p0.rest_4_, ...), custom_call_target="tpu_custom_call" | custom-call | flops 36300001280 | bytes 1024 | tf_op jit(solution)/shard_map/pallas_call | solution.py:504
  75.3 2.6 collective-permute-done.5.f3.r3
  78.9 41.3 %shard_map.266 = (bf16[2048,2048]{1,0:T(8,128)(2,1)}, bf16[2048,512]{1,0:T(8,128)(2,1)}, bf16[2048,512]{1,0:T(8,128)(2,1)}, bf16[2,2048,128]{2,1,0:T(8,128)(2,1)...) custom-call(s32[4]{0:T(128)} %iota_xor_fusion.where, ...), custom_call_target="tpu_custom_call" | custom-call | flops 54999998464 | bytes 1024 | tf_op jit(solution)/shard_map/pallas_call | solution.py:531
  120.8 11.8 %shard_map.267 = (f32[2,64,2048]{2,1,0:T(8,128)}, bf16[1024,128]{1,0:T(8,128)(2,1)}) custom-call(bf16[2,128,2048]{2,1,0:T(8,128)(2,1)} %get-tuple-element.79.dot, bf16[2,2048,128]{2,1,0:T(8,128)(2,1)} %get-tuple-element.80.do, bf16[2,2048,128]{2,1,0:T(8,128)(2,1)} %get-tuple-element.81.q, ...), custom_call_target="tpu_custom_call" | custom-call | flops 12099999744 | bytes 1024 | tf_op jit(solution)/shard_map/pallas_call | solution.py:564
  134.9 29.7 %shard_map.268 = (f32[2,64,2048]{2,1,0:T(8,128)}, bf16[2048,128]{1,0:T(8,128)(2,1)}, bf16[2048,128]{1,0:T(8,128)(2,1)}) custom-call(bf16[2,128,2048]{2,1,0:T(8,128)(2,1)} %get-tuple-element.79.dot, bf16[2,2048,128]{2,1,0:T(8,128)(2,1)} %get-tuple-element.80.do, bf16[2,2048,128]{2,1,0:T(8,128)(2,1)} %get-tuple-element.81.q, ...), custom_call_target="tpu_custom_call", output_to_operand_aliasing={{0}: (3, {})} | custom-call | flops 32999999488 | bytes 1024 | tf_op jit(solution)/shard_map/pallas_call | solution.py:564
  166.2 3.8 %all-to-all-start.2 = ((bf16[8,152,512]{2,1,0:T(8,128)(2,1)}), bf16[8,152,512]{2,1,0:T(8,128)(2,1)S(1)}, u32[]{:S(2)}, u32[]{:S(2)}) async-start(bf16[8,152,512]{2,1,0:T(8,128)(2,1)} %pad_maximum_fusion), calls=%async_computation.2 | async-start | bytes 2490368 | tf_op jit(solution)/shard_map/all_to_all | solution.py:597
  170.0 1.3 collective-permute-start.10
  171.4 38.1 %shard_map.269 = (f32[2,64,2048]{2,1,0:T(8,128)}, bf16[2048,128]{1,0:T(8,128)(2,1)}, bf16[2048,128]{1,0:T(8,128)(2,1)}) custom-call(bf16[2,128,2048]{2,1,0:T(8,128)(2,1)} %get-tuple-element.79.dot, bf16[2,2048,128]{2,1,0:T(8,128)(2,1)} %get-tuple-element.80.do, bf16[2,2048,128]{2,1,0:T(8,128)(2,1)} %get-tuple-element.81.q, ...), custom_call_target="tpu_custom_call", output_to_operand_aliasing={{0}: (3, {})} | custom-call | flops 42900000768 | bytes 1024 | tf_op jit(solution)/shard_map/pallas_call | solution.py:564
  211.7 5.9 %all-to-all-start.3 = ((bf16[8,136,512]{2,1,0:T(8,128)(2,1)}), bf16[8,136,512]{2,1,0:T(8,128)(2,1)S(1)}, u32[]{:S(2)}, u32[]{:S(2)}) async-start(bf16[8,136,512]{2,1,0:T(8,128)(2,1)} %broadcast_in_dim.50), calls=%async_computation.3 | async-start | bytes 2228224 | tf_op jit(solution)/shard_map/all_to_all | solution.py:410
  218.4 8.4 %shard_map.270 = (bf16[2048,512]{1,0:T(8,128)(2,1)}, bf16[176,512]{1,0:T(8,128)(2,1)}, bf16[176,512]{1,0:T(8,128)(2,1)}, bf16[176,512]{1,0:T(8,128)(2,1)}, bf16[176,512]{1,0:T(8,128)(2,1)}) custom-call(s32[4]{0:T(128)} %iota_xor_fusion.where, f32[2,64,2048]{2,1,0:T(8,128)} %get-tuple-element.99.dq, bf16[2048,128]{1,0:T(8,128)(2,1)} %get-tuple-element.100.p0, ...), custom_call_target="tpu_custom_call" | custom-call | flops 11000000512 | bytes 1024 | tf_op jit(solution)/shard_map/pallas_call | solution.py:610
  231.8 11.8 %shard_map.271 = (bf16[2048,512]{1,0:T(8,128)(2,1)}, f32[2048,512]{1,0:T(8,128)}) custom-call(bf16[2048,2048]{1,0:T(8,128)(2,1)} %get-tuple-element.109.active, bf16[2048,512]{1,0:T(8,128)(2,1)} %get-tuple-element.110.middle, bf16[1168,512]{1,0:T(8,128)(2,1)} %copy-done.3, bf16[1168,512]{1,0:T(8,128)(2,1)} %copy-done.13, bf16[1168,512]{1,0:T(8,128)(2,1)} %copy-done.12, ...), custom_call_target="tpu_custom_call" | custom-call | flops 11000000512 | bytes 1024 | tf_op jit(solution)/shard_map/pallas_call | solution.py:632
  243.7 1.3 all-to-all-done.3
  245.8 4.7 %all-to-all-start.4 = ((bf16[8,56,512]{2,1,0:T(8,128)(2,1)}), bf16[8,56,512]{2,1,0:T(8,128)(2,1)S(1)}, u32[]{:S(2)}, u32[]{:S(2)}) async-start(bf16[8,56,512]{2,1,0:T(8,128)(2,1)} %pad_maximum_fusion.2), calls=%async_computation.4 | async-start | bytes 917504 | tf_op jit(solution)/shard_map/all_to_all | solution.py:647
  253.2 1.3 copy.39
  255.7 7.9 %all-to-all-done.4 = bf16[8,56,512]{2,1,0:T(8,128)(2,1)S(1)} async-done(((bf16[8,56,512]{2,1,0:T(8,128)(2,1)}), bf16[8,56,512]{2,1,0:T(8,128)(2,1)S(1)}, u32[]{:S(2)}, u32[]{:S(2)}) %all-to-all-start.4) | async-done | bytes 458784 | tf_op jit(solution)/shard_map/all_to_all | solution.py:647
  (99 shorter events, 23.5 us)
Async XLA Ops:
  0.6 8.9 %copy-start.9 = (bf16[512,8]{0,1:T(8,128)(2,1)S(1)}, bf16[512,8]{0,1:T(8,128)(2,1)}, u32[]{:S(2)}) copy-start(bf16[512,8]{0,1:T(8,128)(2,1)} %param.21) | copy-start | bytes 24580
  2.2 22.9 %all-to-all-start = ((bf16[32,16,512]{2,1,0:T(8,128)(2,1)}), bf16[32,16,512]{2,1,0:T(8,128)(2,1)S(1)}, u32[]{:S(2)}, u32[]{:S(2)}) async-start(bf16[32,16,512]{2,1,0:T(8,128)(2,1)} %broadcast_in_dim.19), calls=%async_computation | async-start | bytes 1048576 | tf_op jit(solution)/shard_map/all_to_all | solution.py:410
  10.2 14.9 %copy-start.8 = (bf16[16,512]{1,0:T(8,128)(2,1)S(1)}, bf16[16,512]{1,0:T(8,128)(2,1)}, u32[]{:S(2)}) copy-start(bf16[16,512]{1,0:T(8,128)(2,1)} %param.24) | copy-start | bytes 49156
  15.4 21.2 %collective-permute-start = (bf16[2048,128]{1,0:T(8,128)(2,1)}, bf16[2048,128]{1,0:T(8,128)(2,1)S(1)}, u32[]{:S(2)}, u32[]{:S(2)}) collective-permute-start(bf16[2048,128]{1,0:T(8,128)(2,1)} %get-tuple-element.69.p0.rest_4_), channel_id=1, source_target_pairs={{0,2},{1,3},{2,0},{3,1},{4,6},{5,7},{6,4},{7,5},{8,10},{9,11},{10,... | collective-permute-start | bytes 1572872 | tf_op jit(solution)/shard_map/ppermute | solution.py:395
  17.1 22.3 %collective-permute-start.1 = (bf16[2048,128]{1,0:T(8,128)(2,1)}, bf16[2048,128]{1,0:T(8,128)(2,1)}, u32[]{:S(2)}, u32[]{:S(2)}) collective-permute-start(bf16[2048,128]{1,0:T(8,128)(2,1)} %get-tuple-element.69.p0.rest_4_), channel_id=1, source_target_pairs={{0,1},{1,0},{2,3},{3,2},{4,5},{5,4},{6,7},{7,6},{8,9},{9,8},{10,11... | collective-permute-start | bytes 1572872 | tf_op jit(solution)/shard_map/ppermute | solution.py:395
  25.8 10.7 %all-to-all-start.1 = ((bf16[8,16,512]{2,1,0:T(8,128)(2,1)}), bf16[8,16,512]{2,1,0:T(8,128)(2,1)S(1)}, u32[]{:S(2)}, u32[]{:S(2)}) async-start(bf16[8,16,512]{2,1,0:T(8,128)(2,1)} %broadcast_in_dim.20), calls=%async_computation.1 | async-start | bytes 262144 | tf_op jit(solution)/shard_map/all_to_all | solution.py:410
  36.6 38.4 %copy-start.3 = (bf16[1168,512]{1,0:T(8,128)(2,1)}, bf16[1168,512]{1,0:T(8,128)(2,1)S(1)}, u32[]{:S(2)}) copy-start(bf16[1168,512]{1,0:T(8,128)(2,1)S(1)} %pad_maximum_fusion.1.f0.r0) | copy-start | bytes 3588100
  36.6 2.9 %collective-permute-start.2 = (bf16[2048,128]{1,0:T(8,128)(2,1)S(1)}, bf16[2048,128]{1,0:T(8,128)(2,1)S(1)}, u32[]{:S(2)}, u32[]{:S(2)}) collective-permute-start(bf16[2048,128]{1,0:T(8,128)(2,1)S(1)} %collective-permute-done.p2.rest_5_), channel_id=1, source_target_pairs={{0,1},{1,0},{2,3},{3,2},{4,5},{5,4},{6,7},{7,6},{8,9},{9,8},{10,11... | collective-permute-start | bytes 1572872 | tf_op jit(solution)/shard_map/ppermute | solution.py:395
  37.9 37.1 %collective-permute-start.4 = (bf16[1168,512]{1,0:T(8,128)(2,1)S(1)}, bf16[1168,512]{1,0:T(8,128)(2,1)S(1)}, u32[]{:S(2)}, u32[]{:S(2)}) collective-permute-start(bf16[1168,512]{1,0:T(8,128)(2,1)S(1)} %pad_maximum_fusion.1.f0.r0), channel_id=1, source_target_pairs={{0,2},{1,3},{2,0},{3,1},{4,6},{5,7},{6,4},{7,5},{8,10},{9,11},{10,... | collective-permute-start | bytes 3588104 | tf_op jit(solution)/shard_map/ppermute | solution.py:395
  39.3 36.1 %collective-permute-start.3 = (bf16[1168,512]{1,0:T(8,128)(2,1)S(1)}, bf16[1168,512]{1,0:T(8,128)(2,1)S(1)}, u32[]{:S(2)}, u32[]{:S(2)}) collective-permute-start(bf16[1168,512]{1,0:T(8,128)(2,1)S(1)} %pad_maximum_fusion.1.f0.r0), channel_id=1, source_target_pairs={{0,1},{1,0},{2,3},{3,2},{4,5},{5,4},{6,7},{7,6},{8,9},{9,8},{10,11... | collective-permute-start | bytes 3588104 | tf_op jit(solution)/shard_map/ppermute | solution.py:395
  74.9 2.9 %collective-permute-start.5 = (bf16[1168,512]{1,0:T(8,128)(2,1)S(1)}, bf16[1168,512]{1,0:T(8,128)(2,1)S(1)}, u32[]{:S(2)}, u32[]{:S(2)}) collective-permute-start(bf16[1168,512]{1,0:T(8,128)(2,1)S(1)} %collective-permute-done.4.f2.r2), channel_id=1, source_target_pairs={{0,1},{1,0},{2,3},{3,2},{4,5},{5,4},{6,7},{7,6},{8,9},{9,8},{10,11... | collective-permute-start | bytes 3588104 | tf_op jit(solution)/shard_map/ppermute | solution.py:395
  120.2 12.3 %collective-permute-start.7 = (bf16[1216,512]{1,0:T(8,128)(2,1)}, bf16[1216,512]{1,0:T(8,128)(2,1)S(1)}, u32[]{:S(2)}, u32[]{:S(2)}) collective-permute-start(bf16[1216,512]{1,0:T(8,128)(2,1)} %get-tuple-element.87), channel_id=1, source_target_pairs={{0,1},{1,0},{2,3},{3,2},{4,5},{5,4},{6,7},{7,6},{8,9},{9,8},{10,11... | collective-permute-start | bytes 3735560 | tf_op jit(solution)/shard_map/ppermute | solution.py:395
  120.6 12.3 %collective-permute-start.6 = (bf16[1216,512]{1,0:T(8,128)(2,1)}, bf16[1216,512]{1,0:T(8,128)(2,1)S(1)}, u32[]{:S(2)}, u32[]{:S(2)}) collective-permute-start(bf16[1216,512]{1,0:T(8,128)(2,1)} %get-tuple-element.85), channel_id=1, source_target_pairs={{0,1},{1,0},{2,3},{3,2},{4,5},{5,4},{6,7},{7,6},{8,9},{9,8},{10,11... | collective-permute-start | bytes 3735560 | tf_op jit(solution)/shard_map/ppermute | solution.py:395
  120.8 11.8 %copy-start.2 = (bf16[1216,512]{1,0:T(8,128)(2,1)S(1)}, bf16[1216,512]{1,0:T(8,128)(2,1)}, u32[]{:S(2)}) copy-start(bf16[1216,512]{1,0:T(8,128)(2,1)} %get-tuple-element.86) | copy-start | bytes 3735556
  134.2 30.4 %collective-permute-start.8 = (bf16[1216,512]{1,0:T(8,128)(2,1)S(1)}, bf16[1216,512]{1,0:T(8,128)(2,1)S(1)}, u32[]{:S(2)}, u32[]{:S(2)}) collective-permute-start(bf16[1216,512]{1,0:T(8,128)(2,1)S(1)} %add_convert_fusion.2), channel_id=1, source_target_pairs={{0,2},{1,3},{2,0},{3,1},{4,6},{5,7},{6,4},{7,5},{8,10},{9,11},{10,... | collective-permute-start | bytes 3735560 | tf_op jit(solution)/shard_map/ppermute | solution.py:395
  166.2 43.4 %all-to-all-start.2 = ((bf16[8,152,512]{2,1,0:T(8,128)(2,1)}), bf16[8,152,512]{2,1,0:T(8,128)(2,1)S(1)}, u32[]{:S(2)}, u32[]{:S(2)}) async-start(bf16[8,152,512]{2,1,0:T(8,128)(2,1)} %pad_maximum_fusion), calls=%async_computation.2 | async-start | bytes 2490368 | tf_op jit(solution)/shard_map/all_to_all | solution.py:597
  170.0 47.6 %collective-permute-start.10 = (bf16[2048,128]{1,0:T(8,128)(2,1)S(1)}, bf16[2048,128]{1,0:T(8,128)(2,1)S(1)}, u32[]{:S(2)}, u32[]{:S(2)}) collective-permute-start(bf16[2048,128]{1,0:T(8,128)(2,1)S(1)} %copy-done.16), channel_id=1, source_target_pairs={{0,2},{1,3},{2,0},{3,1},{4,6},{5,7},{6,4},{7,5},{8,10},{9,11},{10,... | collective-permute-start | bytes 1572872 | tf_op jit(solution)/shard_map/ppermute | solution.py:395
  171.3 46.3 %collective-permute-start.11 = (bf16[2048,128]{1,0:T(8,128)(2,1)S(1)}, bf16[2048,128]{1,0:T(8,128)(2,1)}, u32[]{:S(2)}, u32[]{:S(2)}) collective-permute-start(bf16[2048,128]{1,0:T(8,128)(2,1)S(1)} %copy-done.15), channel_id=1, source_target_pairs={{0,3},{1,2},{2,1},{3,0},{4,7},{5,6},{6,5},{7,4},{8,11},{9,10},{10,... | collective-permute-start | bytes 1572872 | tf_op jit(solution)/shard_map/ppermute | solution.py:395
  209.7 7.9 %collective-permute-start.9 = (bf16[2048,128]{1,0:T(8,128)(2,1)}, bf16[2048,128]{1,0:T(8,128)(2,1)}, u32[]{:S(2)}, u32[]{:S(2)}) collective-permute-start(bf16[2048,128]{1,0:T(8,128)(2,1)} %get-tuple-element.101), channel_id=1, source_target_pairs={{0,1},{1,0},{2,3},{3,2},{4,5},{5,4},{6,7},{7,6},{8,9},{9,8},{10,11... | collective-permute-start | bytes 1572872 | tf_op jit(solution)/shard_map/ppermute | solution.py:395
  211.7 33.3 %all-to-all-start.3 = ((bf16[8,136,512]{2,1,0:T(8,128)(2,1)}), bf16[8,136,512]{2,1,0:T(8,128)(2,1)S(1)}, u32[]{:S(2)}, u32[]{:S(2)}) async-start(bf16[8,136,512]{2,1,0:T(8,128)(2,1)} %broadcast_in_dim.50), calls=%async_computation.3 | async-start | bytes 2228224 | tf_op jit(solution)/shard_map/all_to_all | solution.py:410
  226.9 1.7 collective-permute-start.13
  227.5 3.3 %collective-permute-start.12 = (bf16[176,512]{1,0:T(8,128)(2,1)}, bf16[176,512]{1,0:T(8,128)(2,1)S(1)}, u32[]{:S(2)}, u32[]{:S(2)}) collective-permute-start(bf16[176,512]{1,0:T(8,128)(2,1)} %get-tuple-element.108), channel_id=1, source_target_pairs={{0,1},{1,0},{2,3},{3,2},{4,5},{5,4},{6,7},{7,6},{8,9},{9,8},{10,11... | collective-permute-start | bytes 540680 | tf_op jit(solution)/shard_map/ppermute | solution.py:395
  229.5 14.1 %collective-permute-start.14 = (bf16[176,512]{1,0:T(8,128)(2,1)S(1)}, bf16[176,512]{1,0:T(8,128)(2,1)S(1)}, u32[]{:S(2)}, u32[]{:S(2)}) collective-permute-start(bf16[176,512]{1,0:T(8,128)(2,1)S(1)} %add_convert_fusion.4), channel_id=1, source_target_pairs={{0,2},{1,3},{2,0},{3,1},{4,6},{5,7},{6,4},{7,5},{8,10},{9,11},{10,... | collective-permute-start | bytes 540680 | tf_op jit(solution)/shard_map/ppermute | solution.py:395
  245.8 17.8 %all-to-all-start.4 = ((bf16[8,56,512]{2,1,0:T(8,128)(2,1)}), bf16[8,56,512]{2,1,0:T(8,128)(2,1)S(1)}, u32[]{:S(2)}, u32[]{:S(2)}) async-start(bf16[8,56,512]{2,1,0:T(8,128)(2,1)} %pad_maximum_fusion.2), calls=%async_computation.4 | async-start | bytes 917504 | tf_op jit(solution)/shard_map/all_to_all | solution.py:647
  (14 other events, 55.7 us)

commit v3 on v2

--- a/solution.py
+++ b/solution.py
@@ -333,7 +333,7 @@
 
 def last_kernel(
     where, dq, p0, p1, p2, p3, logit, routes, normed, x, wq, proj, router,
-    out, s0, s1, s2, s3, wq_sum, sp_sum, small, *, head, experts,
+    out, s0, s1, s2, s3, wq_sum, sp_sum, small, turned, *, head, experts,
 ):
     step = pl.program_id(0)
 
@@ -364,6 +364,7 @@
         block = sp_sum.shape[1] // 4
         each = sp_sum.shape[0] // 4
         table = experts * share
+        turned[...] = sp_sum[...].T
         for o, s in enumerate((s0, s1, s2, s3)):
             owner = where[o]
             for e in range(experts):
@@ -376,7 +377,7 @@
                 ends = jnp.where(line == 0, small[g : g + 1, lanes], 0.0)
                 s[table + each : table + each + 16, g * block : (g + 1) * block] = ends.astype(BF)
             for g in range(4):
-                piece = sp_sum[g * each : (g + 1) * each, lanes]
+                piece = turned[pl.ds(pl.multiple_of(owner * block + g * each, each), each), :]
                 s[table : table + each, g * block : (g + 1) * block] = piece.astype(BF)
 
 
@@ -617,7 +618,7 @@
         out_shape=[shape((tokens, width), BF)] + [shape((share + 48, width), BF)] * 4,
         scratch_shapes=[
             pltpu.VMEM((experts * head, width), F32), pltpu.VMEM((2 * head, width), F32),
-            pltpu.VMEM((8, width), F32),
+            pltpu.VMEM((8, width), F32), pltpu.VMEM((width, 2 * head), F32),
         ],
         compiler_params=PARAMS,
         cost_estimate=cost(10),
@@ -660,7 +661,7 @@
         ends[each, :block],
         ends[each, block : 2 * block],
         cut[8 : 8 + experts].T,
-        shared_total.T,
+        shared_total,
         wq_total,
         wo_total,
         cut[1],

time: 266 us -> 266 us (level)
    unnamed x38 -> x37, local copies, waits for them, and re-layouts: 5.6 us -> 4.87 us
  transfers between devices with their start and end apart: 20 -> 20, of which waited for: 6 -> 6; matrix products, arithmetic and copies ran while one was open for 4% -> 4% of each run, Pallas kernels for 54% -> 55%
where the time goes in v3:
time: 266 us
  Pallas kernels  186 us (70%)
  starting transfers between devices  34.4 us (13%)
  waiting for transfers between devices  22.4 us (8%)
  local copies, waits for them, and re-layouts  13.7 us (5%)
  other arithmetic  7.26 us (3%)
    pallas_call x3, Pallas kernels, back_call(): pl.pallas_call(functools.partial(attend_back_kernel, head=head, places=pl...  79.6 us
    pallas_call x1, Pallas kernels, on_device(): pl.pallas_call(functools.partial(middle_kernel, head=head, experts=expert...  41.3 us
    pallas_call x1, Pallas kernels, on_device(): pl.pallas_call(functools.partial(attend_kernel, head=head, span=4 * token...  34.7 us
    all_to_all x3, starting transfers between devices, sent_to_all(): return lax.all_to_all(wide, axes, split_axis=0, concat_axis=0, tiled=True)  16.6 us
    pallas_call x1, Pallas kernels, on_device(): pl.pallas_call(outputs_kernel, grid=(tokens // to,), in_specs=[spec((to,...  11.8 us
    all_to_all x3, waiting for transfers between devices, sent_to_all(): return lax.all_to_all(wide, axes, split_axis=0, concat_axis=0, tiled=True)  11.4 us
    ppermute x15, starting transfers between devices, swapped(): return lax.ppermute(value, 'mp', [(i, i ^ bit) for i in range(4)])  9.21 us
    pallas_call x1, Pallas kernels, on_device(): pl.pallas_call(functools.partial(last_kernel, head=head, experts=experts)...  8.49 us
  transfers between devices with their start and end apart: 20, of which 6 were waited for; matrix products, arithmetic and copies ran while one was open for 4% of the time, Pallas kernels for 55%

profile of v3, /device:TPU:0, one launch (start us, length us, event | category | flops | bytes accessed | tf_op | source)
XLA Modules:
  0.0 265.5 jit_solution(17663846187745965011)
XLA Ops:
  0.7 1.6 broadcast_in_dim.19
  2.2 7.3 %all-to-all-start = ((bf16[32,16,512]{2,1,0:T(8,128)(2,1)}), bf16[32,16,512]{2,1,0:T(8,128)(2,1)S(1)}, u32[]{:S(2)}, u32[]{:S(2)}) async-start(bf16[32,16,512]{2,1,0:T(8,128)(2,1)} %broadcast_in_dim.19), calls=%async_computation | async-start | bytes 1048576 | tf_op jit(solution)/shard_map/all_to_all | solution.py:411
  10.2 5.2 %shard_map.263 = (bf16[2048,512]{1,0:T(8,128)(2,1)}, bf16[2048,128]{1,0:T(8,128)(2,1)}, f32[2,2048]{1,0:T(2,128)}) custom-call(bf16[2048,512]{1,0:T(8,128)(2,1)} %bitcast.48, f32[1,512]{1,0:T(1,128)} %bitcast.59, f32[1,512]{1,0:T(1,128)} %bitcast.56, bf16[16,512]{1,0:T(8,128)(2,1)} %pad.4.router, bf16[512,128]{1,0:T(8,128)(2,1)} %proj.3, s32[2,2048]{1,0:T(2,128)} %bitcast.52), custom_call_target="tpu_custom_call" | custom-call | flops 5500000256 | bytes 1024 | tf_op jit(solution)/shard_map/pallas_call | solution.py:470
  15.4 1.8 collective-permute-start
  17.1 7.9 %all-to-all-done = bf16[32,16,512]{2,1,0:T(8,128)(2,1)S(1)} async-done(((bf16[32,16,512]{2,1,0:T(8,128)(2,1)}), bf16[32,16,512]{2,1,0:T(8,128)(2,1)S(1)}, u32[]{:S(2)}, u32[]{:S(2)}) %all-to-all-start) | async-done | bytes 524320 | tf_op jit(solution)/shard_map/all_to_all | solution.py:411
  25.8 3.4 %all-to-all-start.1 = ((bf16[8,16,512]{2,1,0:T(8,128)(2,1)}), bf16[8,16,512]{2,1,0:T(8,128)(2,1)S(1)}, u32[]{:S(2)}, u32[]{:S(2)}) async-start(bf16[8,16,512]{2,1,0:T(8,128)(2,1)} %broadcast_in_dim.20), calls=%async_computation.1 | async-start | bytes 262144 | tf_op jit(solution)/shard_map/all_to_all | solution.py:411
  29.2 5.1 %shard_map.264 = (bf16[2,64,2048]{2,1,0:T(8,128)(2,1)}, bf16[2,2048,128]{2,1,0:T(8,128)(2,1)}) custom-call(bf16[2048,512]{1,0:T(8,128)(2,1)} %get-tuple-element.70.normed, bf16[512,512]{1,0:T(8,128)(2,1)} %bitcast.42, s32[2,2048]{1,0:T(2,128)} %bitcast.53), custom_call_target="tpu_custom_call" | custom-call | flops 5500000256 | bytes 1024 | tf_op jit(solution)/shard_map/pallas_call | solution.py:487
  34.3 2.2 all-to-all-done.1
  37.9 1.4 collective-permute-start.4
  40.3 34.7 %shard_map.265 = (f32[2,72,2048]{2,1,0:T(8,128)}, bf16[8192,4096]{1,0:T(8,128)(2,1)}) custom-call(s32[4]{0:T(128)} %iota_xor_fusion.where, s32[1]{0:T(128)S(6)} %copy.39.length, bf16[2,64,2048]{2,1,0:T(8,128)(2,1)} %get-tuple-element.73.q, bf16[2048,128]{1,0:T(8,128)(2,1)} %get-tuple-element.69.p0.rest_4_, ...), custom_call_target="tpu_custom_call" | custom-call | flops 36300001280 | bytes 1024 | tf_op jit(solution)/shard_map/pallas_call | solution.py:505
  75.3 2.6 collective-permute-done.5.f3.r3
  78.9 41.3 %shard_map.266 = (bf16[2048,2048]{1,0:T(8,128)(2,1)}, bf16[2048,512]{1,0:T(8,128)(2,1)}, bf16[2048,512]{1,0:T(8,128)(2,1)}, bf16[2,2048,128]{2,1,0:T(8,128)(2,1)...) custom-call(s32[4]{0:T(128)} %iota_xor_fusion.where, ...), custom_call_target="tpu_custom_call" | custom-call | flops 54999998464 | bytes 1024 | tf_op jit(solution)/shard_map/pallas_call | solution.py:532
  120.8 11.8 %shard_map.267 = (f32[2,64,2048]{2,1,0:T(8,128)}, bf16[1024,128]{1,0:T(8,128)(2,1)}) custom-call(bf16[2,128,2048]{2,1,0:T(8,128)(2,1)} %get-tuple-element.79.dot, bf16[2,2048,128]{2,1,0:T(8,128)(2,1)} %get-tuple-element.80.do, bf16[2,2048,128]{2,1,0:T(8,128)(2,1)} %get-tuple-element.81.q, ...), custom_call_target="tpu_custom_call" | custom-call | flops 12099999744 | bytes 1024 | tf_op jit(solution)/shard_map/pallas_call | solution.py:565
  134.9 29.7 %shard_map.268 = (f32[2,64,2048]{2,1,0:T(8,128)}, bf16[2048,128]{1,0:T(8,128)(2,1)}, bf16[2048,128]{1,0:T(8,128)(2,1)}) custom-call(bf16[2,128,2048]{2,1,0:T(8,128)(2,1)} %get-tuple-element.79.dot, bf16[2,2048,128]{2,1,0:T(8,128)(2,1)} %get-tuple-element.80.do, bf16[2,2048,128]{2,1,0:T(8,128)(2,1)} %get-tuple-element.81.q, ...), custom_call_target="tpu_custom_call", output_to_operand_aliasing={{0}: (3, {})} | custom-call | flops 32999999488 | bytes 1024 | tf_op jit(solution)/shard_map/pallas_call | solution.py:565
  166.2 3.8 %all-to-all-start.2 = ((bf16[8,152,512]{2,1,0:T(8,128)(2,1)}), bf16[8,152,512]{2,1,0:T(8,128)(2,1)S(1)}, u32[]{:S(2)}, u32[]{:S(2)}) async-start(bf16[8,152,512]{2,1,0:T(8,128)(2,1)} %pad_maximum_fusion), calls=%async_computation.2 | async-start | bytes 2490368 | tf_op jit(solution)/shard_map/all_to_all | solution.py:598
  170.0 1.3 collective-permute-start.10
  171.4 38.1 %shard_map.269 = (f32[2,64,2048]{2,1,0:T(8,128)}, bf16[2048,128]{1,0:T(8,128)(2,1)}, bf16[2048,128]{1,0:T(8,128)(2,1)}) custom-call(bf16[2,128,2048]{2,1,0:T(8,128)(2,1)} %get-tuple-element.79.dot, bf16[2,2048,128]{2,1,0:T(8,128)(2,1)} %get-tuple-element.80.do, bf16[2,2048,128]{2,1,0:T(8,128)(2,1)} %get-tuple-element.81.q, ...), custom_call_target="tpu_custom_call", output_to_operand_aliasing={{0}: (3, {})} | custom-call | flops 42900000768 | bytes 1024 | tf_op jit(solution)/shard_map/pallas_call | solution.py:565
  211.7 5.9 %all-to-all-start.3 = ((bf16[8,136,512]{2,1,0:T(8,128)(2,1)}), bf16[8,136,512]{2,1,0:T(8,128)(2,1)S(1)}, u32[]{:S(2)}, u32[]{:S(2)}) async-start(bf16[8,136,512]{2,1,0:T(8,128)(2,1)} %broadcast_in_dim.50), calls=%async_computation.3 | async-start | bytes 2228224 | tf_op jit(solution)/shard_map/all_to_all | solution.py:411
  218.4 8.5 %shard_map.270 = (bf16[2048,512]{1,0:T(8,128)(2,1)}, bf16[176,512]{1,0:T(8,128)(2,1)}, bf16[176,512]{1,0:T(8,128)(2,1)}, bf16[176,512]{1,0:T(8,128)(2,1)}, bf16[176,512]{1,0:T(8,128)(2,1)}) custom-call(s32[4]{0:T(128)} %iota_xor_fusion.where, f32[2,64,2048]{2,1,0:T(8,128)} %get-tuple-element.99.dq, bf16[2048,128]{1,0:T(8,128)(2,1)} %get-tuple-element.100.p0, ...), custom_call_target="tpu_custom_call" | custom-call | flops 11000000512 | bytes 1024 | tf_op jit(solution)/shard_map/pallas_call | solution.py:611
  229.6 1.3 collective-permute-start.14
  231.9 11.8 %shard_map.271 = (bf16[2048,512]{1,0:T(8,128)(2,1)}, f32[2048,512]{1,0:T(8,128)}) custom-call(bf16[2048,2048]{1,0:T(8,128)(2,1)} %get-tuple-element.109.active, bf16[2048,512]{1,0:T(8,128)(2,1)} %get-tuple-element.110.middle, bf16[1168,512]{1,0:T(8,128)(2,1)} %copy-done.3, bf16[1168,512]{1,0:T(8,128)(2,1)} %copy-done.13, bf16[1168,512]{1,0:T(8,128)(2,1)} %copy-done.12, ...), custom_call_target="tpu_custom_call" | custom-call | flops 11000000512 | bytes 1024 | tf_op jit(solution)/shard_map/pallas_call | solution.py:633
  245.8 4.7 %all-to-all-start.4 = ((bf16[8,56,512]{2,1,0:T(8,128)(2,1)}), bf16[8,56,512]{2,1,0:T(8,128)(2,1)S(1)}, u32[]{:S(2)}, u32[]{:S(2)}) async-start(bf16[8,56,512]{2,1,0:T(8,128)(2,1)} %pad_maximum_fusion.2), calls=%async_computation.4 | async-start | bytes 917504 | tf_op jit(solution)/shard_map/all_to_all | solution.py:648
  253.3 1.3 copy.36
  255.8 7.9 %all-to-all-done.4 = bf16[8,56,512]{2,1,0:T(8,128)(2,1)S(1)} async-done(((bf16[8,56,512]{2,1,0:T(8,128)(2,1)}), bf16[8,56,512]{2,1,0:T(8,128)(2,1)S(1)}, u32[]{:S(2)}, u32[]{:S(2)}) %all-to-all-start.4) | async-done | bytes 458784 | tf_op jit(solution)/shard_map/all_to_all | solution.py:648
  (98 shorter events, 23.3 us)
Async XLA Ops:
  0.6 8.9 %copy-start.9 = (bf16[512,8]{0,1:T(8,128)(2,1)S(1)}, bf16[512,8]{0,1:T(8,128)(2,1)}, u32[]{:S(2)}) copy-start(bf16[512,8]{0,1:T(8,128)(2,1)} %param.21) | copy-start | bytes 24580
  2.2 22.9 %all-to-all-start = ((bf16[32,16,512]{2,1,0:T(8,128)(2,1)}), bf16[32,16,512]{2,1,0:T(8,128)(2,1)S(1)}, u32[]{:S(2)}, u32[]{:S(2)}) async-start(bf16[32,16,512]{2,1,0:T(8,128)(2,1)} %broadcast_in_dim.19), calls=%async_computation | async-start | bytes 1048576 | tf_op jit(solution)/shard_map/all_to_all | solution.py:411
  10.2 14.9 %copy-start.8 = (bf16[16,512]{1,0:T(8,128)(2,1)S(1)}, bf16[16,512]{1,0:T(8,128)(2,1)}, u32[]{:S(2)}) copy-start(bf16[16,512]{1,0:T(8,128)(2,1)} %param.24) | copy-start | bytes 49156
  15.4 21.2 %collective-permute-start = (bf16[2048,128]{1,0:T(8,128)(2,1)}, bf16[2048,128]{1,0:T(8,128)(2,1)S(1)}, u32[]{:S(2)}, u32[]{:S(2)}) collective-permute-start(bf16[2048,128]{1,0:T(8,128)(2,1)} %get-tuple-element.69.p0.rest_4_), channel_id=1, source_target_pairs={{0,2},{1,3},{2,0},{3,1},{4,6},{5,7},{6,4},{7,5},{8,10},{9,11},{10,... | collective-permute-start | bytes 1572872 | tf_op jit(solution)/shard_map/ppermute | solution.py:396
  17.1 22.3 %collective-permute-start.1 = (bf16[2048,128]{1,0:T(8,128)(2,1)}, bf16[2048,128]{1,0:T(8,128)(2,1)}, u32[]{:S(2)}, u32[]{:S(2)}) collective-permute-start(bf16[2048,128]{1,0:T(8,128)(2,1)} %get-tuple-element.69.p0.rest_4_), channel_id=1, source_target_pairs={{0,1},{1,0},{2,3},{3,2},{4,5},{5,4},{6,7},{7,6},{8,9},{9,8},{10,11... | collective-permute-start | bytes 1572872 | tf_op jit(solution)/shard_map/ppermute | solution.py:396
  25.8 10.7 %all-to-all-start.1 = ((bf16[8,16,512]{2,1,0:T(8,128)(2,1)}), bf16[8,16,512]{2,1,0:T(8,128)(2,1)S(1)}, u32[]{:S(2)}, u32[]{:S(2)}) async-start(bf16[8,16,512]{2,1,0:T(8,128)(2,1)} %broadcast_in_dim.20), calls=%async_computation.1 | async-start | bytes 262144 | tf_op jit(solution)/shard_map/all_to_all | solution.py:411
  36.6 38.4 %copy-start.3 = (bf16[1168,512]{1,0:T(8,128)(2,1)}, bf16[1168,512]{1,0:T(8,128)(2,1)S(1)}, u32[]{:S(2)}) copy-start(bf16[1168,512]{1,0:T(8,128)(2,1)S(1)} %pad_maximum_fusion.1.f0.r0) | copy-start | bytes 3588100
  36.6 2.9 %collective-permute-start.2 = (bf16[2048,128]{1,0:T(8,128)(2,1)S(1)}, bf16[2048,128]{1,0:T(8,128)(2,1)S(1)}, u32[]{:S(2)}, u32[]{:S(2)}) collective-permute-start(bf16[2048,128]{1,0:T(8,128)(2,1)S(1)} %collective-permute-done.p2.rest_5_), channel_id=1, source_target_pairs={{0,1},{1,0},{2,3},{3,2},{4,5},{5,4},{6,7},{7,6},{8,9},{9,8},{10,11... | collective-permute-start | bytes 1572872 | tf_op jit(solution)/shard_map/ppermute | solution.py:396
  37.9 37.1 %collective-permute-start.4 = (bf16[1168,512]{1,0:T(8,128)(2,1)S(1)}, bf16[1168,512]{1,0:T(8,128)(2,1)S(1)}, u32[]{:S(2)}, u32[]{:S(2)}) collective-permute-start(bf16[1168,512]{1,0:T(8,128)(2,1)S(1)} %pad_maximum_fusion.1.f0.r0), channel_id=1, source_target_pairs={{0,2},{1,3},{2,0},{3,1},{4,6},{5,7},{6,4},{7,5},{8,10},{9,11},{10,... | collective-permute-start | bytes 3588104 | tf_op jit(solution)/shard_map/ppermute | solution.py:396
  39.3 36.1 %collective-permute-start.3 = (bf16[1168,512]{1,0:T(8,128)(2,1)S(1)}, bf16[1168,512]{1,0:T(8,128)(2,1)S(1)}, u32[]{:S(2)}, u32[]{:S(2)}) collective-permute-start(bf16[1168,512]{1,0:T(8,128)(2,1)S(1)} %pad_maximum_fusion.1.f0.r0), channel_id=1, source_target_pairs={{0,1},{1,0},{2,3},{3,2},{4,5},{5,4},{6,7},{7,6},{8,9},{9,8},{10,11... | collective-permute-start | bytes 3588104 | tf_op jit(solution)/shard_map/ppermute | solution.py:396
  74.9 2.9 %collective-permute-start.5 = (bf16[1168,512]{1,0:T(8,128)(2,1)S(1)}, bf16[1168,512]{1,0:T(8,128)(2,1)S(1)}, u32[]{:S(2)}, u32[]{:S(2)}) collective-permute-start(bf16[1168,512]{1,0:T(8,128)(2,1)S(1)} %collective-permute-done.4.f2.r2), channel_id=1, source_target_pairs={{0,1},{1,0},{2,3},{3,2},{4,5},{5,4},{6,7},{7,6},{8,9},{9,8},{10,11... | collective-permute-start | bytes 3588104 | tf_op jit(solution)/shard_map/ppermute | solution.py:396
  120.2 12.3 %collective-permute-start.7 = (bf16[1216,512]{1,0:T(8,128)(2,1)}, bf16[1216,512]{1,0:T(8,128)(2,1)S(1)}, u32[]{:S(2)}, u32[]{:S(2)}) collective-permute-start(bf16[1216,512]{1,0:T(8,128)(2,1)} %get-tuple-element.87), channel_id=1, source_target_pairs={{0,1},{1,0},{2,3},{3,2},{4,5},{5,4},{6,7},{7,6},{8,9},{9,8},{10,11... | collective-permute-start | bytes 3735560 | tf_op jit(solution)/shard_map/ppermute | solution.py:396
  120.6 12.3 %collective-permute-start.6 = (bf16[1216,512]{1,0:T(8,128)(2,1)}, bf16[1216,512]{1,0:T(8,128)(2,1)S(1)}, u32[]{:S(2)}, u32[]{:S(2)}) collective-permute-start(bf16[1216,512]{1,0:T(8,128)(2,1)} %get-tuple-element.85), channel_id=1, source_target_pairs={{0,1},{1,0},{2,3},{3,2},{4,5},{5,4},{6,7},{7,6},{8,9},{9,8},{10,11... | collective-permute-start | bytes 3735560 | tf_op jit(solution)/shard_map/ppermute | solution.py:396
  120.8 11.8 %copy-start.2 = (bf16[1216,512]{1,0:T(8,128)(2,1)S(1)}, bf16[1216,512]{1,0:T(8,128)(2,1)}, u32[]{:S(2)}) copy-start(bf16[1216,512]{1,0:T(8,128)(2,1)} %get-tuple-element.86) | copy-start | bytes 3735556
  134.2 30.4 %collective-permute-start.8 = (bf16[1216,512]{1,0:T(8,128)(2,1)S(1)}, bf16[1216,512]{1,0:T(8,128)(2,1)S(1)}, u32[]{:S(2)}, u32[]{:S(2)}) collective-permute-start(bf16[1216,512]{1,0:T(8,128)(2,1)S(1)} %add_convert_fusion.2), channel_id=1, source_target_pairs={{0,2},{1,3},{2,0},{3,1},{4,6},{5,7},{6,4},{7,5},{8,10},{9,11},{10,... | collective-permute-start | bytes 3735560 | tf_op jit(solution)/shard_map/ppermute | solution.py:396
  166.2 43.4 %all-to-all-start.2 = ((bf16[8,152,512]{2,1,0:T(8,128)(2,1)}), bf16[8,152,512]{2,1,0:T(8,128)(2,1)S(1)}, u32[]{:S(2)}, u32[]{:S(2)}) async-start(bf16[8,152,512]{2,1,0:T(8,128)(2,1)} %pad_maximum_fusion), calls=%async_computation.2 | async-start | bytes 2490368 | tf_op jit(solution)/shard_map/all_to_all | solution.py:598
  170.0 47.6 %collective-permute-start.10 = (bf16[2048,128]{1,0:T(8,128)(2,1)S(1)}, bf16[2048,128]{1,0:T(8,128)(2,1)S(1)}, u32[]{:S(2)}, u32[]{:S(2)}) collective-permute-start(bf16[2048,128]{1,0:T(8,128)(2,1)S(1)} %copy-done.16), channel_id=1, source_target_pairs={{0,2},{1,3},{2,0},{3,1},{4,6},{5,7},{6,4},{7,5},{8,10},{9,11},{10,... | collective-permute-start | bytes 1572872 | tf_op jit(solution)/shard_map/ppermute | solution.py:396
  171.3 46.3 %collective-permute-start.11 = (bf16[2048,128]{1,0:T(8,128)(2,1)S(1)}, bf16[2048,128]{1,0:T(8,128)(2,1)}, u32[]{:S(2)}, u32[]{:S(2)}) collective-permute-start(bf16[2048,128]{1,0:T(8,128)(2,1)S(1)} %copy-done.15), channel_id=1, source_target_pairs={{0,3},{1,2},{2,1},{3,0},{4,7},{5,6},{6,5},{7,4},{8,11},{9,10},{10,... | collective-permute-start | bytes 1572872 | tf_op jit(solution)/shard_map/ppermute | solution.py:396
  209.7 7.9 %collective-permute-start.9 = (bf16[2048,128]{1,0:T(8,128)(2,1)}, bf16[2048,128]{1,0:T(8,128)(2,1)}, u32[]{:S(2)}, u32[]{:S(2)}) collective-permute-start(bf16[2048,128]{1,0:T(8,128)(2,1)} %get-tuple-element.101), channel_id=1, source_target_pairs={{0,1},{1,0},{2,3},{3,2},{4,5},{5,4},{6,7},{7,6},{8,9},{9,8},{10,11... | collective-permute-start | bytes 1572872 | tf_op jit(solution)/shard_map/ppermute | solution.py:396
  211.7 33.3 %all-to-all-start.3 = ((bf16[8,136,512]{2,1,0:T(8,128)(2,1)}), bf16[8,136,512]{2,1,0:T(8,128)(2,1)S(1)}, u32[]{:S(2)}, u32[]{:S(2)}) async-start(bf16[8,136,512]{2,1,0:T(8,128)(2,1)} %broadcast_in_dim.50), calls=%async_computation.3 | async-start | bytes 2228224 | tf_op jit(solution)/shard_map/all_to_all | solution.py:411
  226.9 1.7 collective-permute-start.13
  227.6 3.3 %collective-permute-start.12 = (bf16[176,512]{1,0:T(8,128)(2,1)}, bf16[176,512]{1,0:T(8,128)(2,1)S(1)}, u32[]{:S(2)}, u32[]{:S(2)}) collective-permute-start(bf16[176,512]{1,0:T(8,128)(2,1)} %get-tuple-element.108), channel_id=1, source_target_pairs={{0,1},{1,0},{2,3},{3,2},{4,5},{5,4},{6,7},{7,6},{8,9},{9,8},{10,11... | collective-permute-start | bytes 540680 | tf_op jit(solution)/shard_map/ppermute | solution.py:396
  229.6 14.1 %collective-permute-start.14 = (bf16[176,512]{1,0:T(8,128)(2,1)S(1)}, bf16[176,512]{1,0:T(8,128)(2,1)S(1)}, u32[]{:S(2)}, u32[]{:S(2)}) collective-permute-start(bf16[176,512]{1,0:T(8,128)(2,1)S(1)} %add_convert_fusion.4), channel_id=1, source_target_pairs={{0,2},{1,3},{2,0},{3,1},{4,6},{5,7},{6,4},{7,5},{8,10},{9,11},{10,... | collective-permute-start | bytes 540680 | tf_op jit(solution)/shard_map/ppermute | solution.py:396
  245.8 17.9 %all-to-all-start.4 = ((bf16[8,56,512]{2,1,0:T(8,128)(2,1)}), bf16[8,56,512]{2,1,0:T(8,128)(2,1)S(1)}, u32[]{:S(2)}, u32[]{:S(2)}) async-start(bf16[8,56,512]{2,1,0:T(8,128)(2,1)} %pad_maximum_fusion.2), calls=%async_computation.4 | async-start | bytes 917504 | tf_op jit(solution)/shard_map/all_to_all | solution.py:648
  (14 other events, 55.8 us)
